TPU v7x, 128 devices: a whole 4x4x4 slice. The times are simulated.
128 devices in a mesh: dp: 32 (over y, z, x_lo), tensor: 4 (over x_hi, core).
Axes of the slice: x: 4 (x_hi: 2, x_lo: 2; x = x_hi * 2 + x_lo), y: 4, z: 4, core: 2. Of those that a mesh axis runs over, the one named last changes fastest.
Arguments:
- tokens: bfloat16 [12608, 768], P('dp'), may hold values from -6 to 6
- norm_gain: float32 [4, 768], replicated, may hold values from 0.5 to 1.5
- norm_bias: float32 [4, 768], replicated, may hold values from -1.5 to 1.5
- attn_in: bfloat16 [2, 3, 768, 768], P(None, None, None, 'tensor'), may hold values from -0.21875 to 0.21875
- attn_out: bfloat16 [2, 768, 768], P(None, 'tensor'), may hold values from -0.75 to 0.75
- mlp_in: bfloat16 [768, 3072], P(None, 'tensor'), may hold values from -0.21875 to 0.21875
- mlp_out: bfloat16 [3072, 768], P('tensor'), may hold values from -0.109375 to 0.109375
- expert_in: bfloat16 [4, 768, 3072], P(None, None, 'tensor'), may hold values from -0.21875 to 0.21875
- expert_out: bfloat16 [4, 3072, 768], P(None, 'tensor'), may hold values from -0.109375 to 0.109375
- routes: int32 [12608, 2], P('dp'), may hold values from 0 to 3, as said below
- slot_index: int32 [12608, 2], P('dp'), may hold values from 0 to 168, as said below
- gate_weights: float32 [12608, 2], P('dp'), may hold values from 0.2 to 0.8
- cotangent: bfloat16 [12608, 768], P('dp'), may hold values from -6 to 6
Outputs:
- output: float32 [12608, 768], P('dp')
- token_grad: float32 [12608, 768], P('dp')
- norm_gain_grad: float32 [4, 768], P(None, 'dp')
- norm_bias_grad: float32 [4, 768], P(None, 'dp')
- attn_in_grad: float32 [2, 3, 768, 768], P(None, None, 'dp', 'tensor')
- attn_out_grad: float32 [2, 768, 768], P(None, 'tensor', 'dp')
- mlp_in_grad: float32 [768, 3072], P('dp', 'tensor')
- mlp_out_grad: float32 [3072, 768], P('tensor', 'dp')
- expert_in_grad: float32 [4, 768, 3072], P(None, 'dp', 'tensor')
- expert_out_grad: float32 [4, 3072, 768], P(None, 'tensor', 'dp')
Inputs may be any that keep to these rules, and one draw needn't show every extreme that they name: `routes`: each row names two different experts. `slot_index`: within each aligned block of 394 rows (the rows of one index of dp) and for each expert, the choices that name it, first choices of all rows in row order and then second choices in row order, take slots 0, 1, 2 and so on up to 167; all later ones take 168, which marks a dropped choice; in every block some expert has more than 168 choices.
All inputs are finite; a program needn't handle non-finite values.
Results may differ from a plain program's by a relative error of at most 0.025.
Values may be sent and summed in bfloat16 or wider, within the bound.
A program may use at most 128 MiB of HBM per device.

v0:
```python
import math

import jax
import jax.numpy as jnp
from jax import lax
from jax.sharding import PartitionSpec as P

HEAD_DIM = 64
SEQ = 197
CAPACITY = 168


NORM_EPSILON = 1e-06


def layer_norm(values, gain_row, bias_row):
    center = values - jnp.mean(values, axis=-1, keepdims=True)
    spread = jnp.mean(center * center, axis=-1, keepdims=True)
    return center * lax.rsqrt(spread + NORM_EPSILON) * gain_row + bias_row


def norm_backward(values, gain_row, bias_row, upstream):
    unused, pullback = jax.vjp(layer_norm, values, gain_row, bias_row)
    return pullback(upstream)


def gelu_exact(values):
    return jax.nn.gelu(values, approximate=False)


def head_scores(shaped):
    scaling = 1.0 / math.sqrt(HEAD_DIM)
    return (
        jnp.einsum("bqhd,bkhd->bhqk", shaped[0], shaped[1], preferred_element_type=jnp.float32)
        * scaling
    )


def head_forward(normed, weight_in, weight_out):
    projected = jnp.einsum(
        "nd,jde->jne", normed, weight_in, preferred_element_type=jnp.float32
    ).astype(jnp.bfloat16)
    images = normed.shape[0] // SEQ
    local_heads = weight_in.shape[2] // HEAD_DIM
    shaped = projected.reshape(3, images, SEQ, local_heads, HEAD_DIM)
    scores = head_scores(shaped)
    highest = jnp.max(scores, axis=-1, keepdims=True)
    log_total = highest + jnp.log(jnp.sum(jnp.exp(scores - highest), axis=-1, keepdims=True))
    weights = jnp.exp(scores - log_total).astype(jnp.bfloat16)
    mixture = jnp.einsum("bhqk,bkhd->bqhd", weights, shaped[2], preferred_element_type=jnp.float32)
    mixture = mixture.astype(jnp.bfloat16).reshape(normed.shape[0], weight_in.shape[2])
    partial_sum = jnp.dot(mixture, weight_out, preferred_element_type=jnp.float32)
    mixed_total = lax.psum(partial_sum, "tensor")
    return (mixed_total, (shaped, log_total, mixture))


def head_backward(normed, weight_in, weight_out, stored, upstream):
    shaped, log_total, mixture = stored
    scaling = 1.0 / math.sqrt(HEAD_DIM)
    upstream_low = upstream.astype(jnp.bfloat16)
    grad_out = jnp.einsum("ne,nd->ed", mixture, upstream_low, preferred_element_type=jnp.float32)
    d_mixture = jnp.einsum(
        "nd,ed->ne", upstream_low, weight_out, preferred_element_type=jnp.float32
    ).astype(jnp.bfloat16)
    d_mixture = d_mixture.reshape(shaped.shape[1:])
    probability = jnp.exp(head_scores(shaped) - log_total)
    d_weights = jnp.einsum(
        "bqhd,bkhd->bhqk", d_mixture, shaped[2], preferred_element_type=jnp.float32
    )
    centered = d_weights - jnp.sum(probability * d_weights, axis=-1, keepdims=True)
    d_scores = (probability * centered).astype(jnp.bfloat16)
    d_query = (
        jnp.einsum("bhqk,bkhd->bqhd", d_scores, shaped[1], preferred_element_type=jnp.float32)
        * scaling
    ).astype(jnp.bfloat16)
    d_keys = (
        jnp.einsum("bhqk,bqhd->bkhd", d_scores, shaped[0], preferred_element_type=jnp.float32)
        * scaling
    ).astype(jnp.bfloat16)
    d_values = jnp.einsum(
        "bhqk,bqhd->bkhd",
        probability.astype(jnp.bfloat16),
        d_mixture,
        preferred_element_type=jnp.float32,
    ).astype(jnp.bfloat16)
    d_projected = jnp.stack([d_query, d_keys, d_values]).reshape(
        3, normed.shape[0], weight_in.shape[2]
    )
    grad_in = jnp.einsum("nd,jne->jde", normed, d_projected, preferred_element_type=jnp.float32)
    d_normed = jnp.einsum("jne,jde->nd", d_projected, weight_in, preferred_element_type=jnp.float32)
    return (
        lax.psum(d_normed.astype(jnp.bfloat16), "tensor").astype(jnp.float32),
        grad_in,
        grad_out,
    )


def dense_forward(normed, weight_in, weight_out):
    hidden = jnp.dot(normed, weight_in, preferred_element_type=jnp.float32)
    active = gelu_exact(hidden).astype(jnp.bfloat16)
    partial_sum = jnp.dot(active, weight_out, preferred_element_type=jnp.float32)
    return (
        lax.psum(partial_sum.astype(jnp.bfloat16), "tensor").astype(jnp.float32),
        (hidden, active),
    )


def dense_backward(normed, weight_in, weight_out, stored, upstream):
    hidden, active = stored
    upstream_low = upstream.astype(jnp.bfloat16)
    grad_out = jnp.einsum("nf,nd->fd", active, upstream_low, preferred_element_type=jnp.float32)
    d_active = jnp.einsum("nd,fd->nf", upstream_low, weight_out, preferred_element_type=jnp.float32)
    unused, pullback = jax.vjp(gelu_exact, hidden)
    d_hidden = pullback(d_active)[0].astype(jnp.bfloat16)
    grad_in = jnp.einsum("nd,nf->df", normed, d_hidden, preferred_element_type=jnp.float32)
    d_normed = jnp.einsum("nf,df->nd", d_hidden, weight_in, preferred_element_type=jnp.float32)
    return (
        lax.psum(d_normed.astype(jnp.bfloat16), "tensor").astype(jnp.float32),
        grad_in,
        grad_out,
    )


def expert_tables(routes, slot_index, gate_weights, expert_count):
    row_count = routes.shape[0]
    kept_mask = slot_index < CAPACITY
    token_ids = jnp.broadcast_to(jnp.arange(row_count, dtype=jnp.int32)[:, None], routes.shape)
    owner_table = (
        jnp.full((expert_count, CAPACITY + 1), row_count, jnp.int32)
        .at[routes, slot_index]
        .set(token_ids)[:, :CAPACITY]
    )
    gate_kept = jnp.where(kept_mask, gate_weights, 0.0)
    gate_table = (
        jnp.zeros((expert_count, CAPACITY + 1), jnp.float32)
        .at[routes, slot_index]
        .set(gate_kept)[:, :CAPACITY]
    )
    flat_index = jnp.where(kept_mask, routes * CAPACITY + slot_index, expert_count * CAPACITY)
    return (owner_table, gate_table, flat_index, gate_kept)


def expert_forward(normed, weight_in, weight_out, tables):
    owner_table, gate_table, flat_index, gate_kept = tables
    width = normed.shape[1]
    padded = jnp.concatenate([normed, jnp.zeros((1, width), normed.dtype)], axis=0)
    buffer = padded[owner_table]
    hidden = jnp.einsum("ecd,edf->ecf", buffer, weight_in, preferred_element_type=jnp.float32)
    active = gelu_exact(hidden).astype(jnp.bfloat16)
    expert_rows = jnp.einsum("ecf,efd->ecd", active, weight_out, preferred_element_type=jnp.float32)
    expert_flat = expert_rows.reshape(-1, width)
    stored = (buffer, hidden, active)
    flat_rows = jnp.concatenate([expert_flat, jnp.zeros((1, width), jnp.float32)], axis=0)
    picked = flat_rows[flat_index]
    partial_sum = jnp.sum(picked * gate_kept[:, :, None], axis=1)
    return (lax.psum(partial_sum.astype(jnp.bfloat16), "tensor").astype(jnp.float32), stored)


def expert_backward(normed, weight_in, weight_out, tables, stored, upstream):
    owner_table, gate_table, flat_index, gate_kept = tables
    inputs_kept, hidden, active = stored
    width = normed.shape[1]
    padded = jnp.concatenate([upstream, jnp.zeros((1, width), jnp.float32)], axis=0)
    d_rows = (padded[owner_table] * gate_table[:, :, None]).astype(jnp.bfloat16)
    grad_out = jnp.einsum("ecf,ecd->efd", active, d_rows, preferred_element_type=jnp.float32)
    d_active = jnp.einsum("ecd,efd->ecf", d_rows, weight_out, preferred_element_type=jnp.float32)
    unused, pullback = jax.vjp(gelu_exact, hidden)
    d_hidden = pullback(d_active)[0].astype(jnp.bfloat16)
    grad_in = jnp.einsum("ecd,ecf->edf", inputs_kept, d_hidden, preferred_element_type=jnp.float32)
    d_buffer = jnp.einsum("ecf,edf->ecd", d_hidden, weight_in, preferred_element_type=jnp.float32)
    d_flat = d_buffer.reshape(-1, width)
    flat_back = jnp.concatenate([d_flat, jnp.zeros((1, width), jnp.float32)], axis=0)
    d_normed = jnp.sum(flat_back[flat_index], axis=1)
    return (
        lax.psum(d_normed.astype(jnp.bfloat16), "tensor").astype(jnp.float32),
        grad_in,
        grad_out,
    )


def local(
    tokens,
    norm_gain,
    norm_bias,
    attn_in,
    attn_out,
    mlp_in,
    mlp_out,
    expert_in,
    expert_out,
    routes,
    slot_index,
    gate_weights,
    cotangent,
):
    stream_a = tokens.astype(jnp.float32)
    normed_a = layer_norm(stream_a, norm_gain[0], norm_bias[0]).astype(jnp.bfloat16)
    mixed_a, stored_a = head_forward(normed_a, attn_in[0], attn_out[0])
    stream_b = stream_a + mixed_a
    normed_b = layer_norm(stream_b, norm_gain[1], norm_bias[1]).astype(jnp.bfloat16)
    mixed_b, stored_b = dense_forward(normed_b, mlp_in, mlp_out)
    stream_c = stream_b + mixed_b
    normed_c = layer_norm(stream_c, norm_gain[2], norm_bias[2]).astype(jnp.bfloat16)
    mixed_c, stored_c = head_forward(normed_c, attn_in[1], attn_out[1])
    stream_d = stream_c + mixed_c
    normed_d = layer_norm(stream_d, norm_gain[3], norm_bias[3]).astype(jnp.bfloat16)
    tables = expert_tables(routes, slot_index, gate_weights, expert_in.shape[0])
    mixed_d, stored_d = expert_forward(normed_d, expert_in, expert_out, tables)
    output = stream_d + mixed_d
    upstream = cotangent.astype(jnp.float32)
    d_normed, grad_ein, grad_eout = expert_backward(
        normed_d, expert_in, expert_out, tables, stored_d, upstream
    )
    d_stream, gain_d, bias_d = norm_backward(stream_d, norm_gain[3], norm_bias[3], d_normed)
    upstream = upstream + d_stream
    d_normed, grad_qkv_c, grad_proj_c = head_backward(
        normed_c, attn_in[1], attn_out[1], stored_c, upstream
    )
    d_stream, gain_c, bias_c = norm_backward(stream_c, norm_gain[2], norm_bias[2], d_normed)
    upstream = upstream + d_stream
    d_normed, grad_mlp_in, grad_mlp_out = dense_backward(
        normed_b, mlp_in, mlp_out, stored_b, upstream
    )
    d_stream, gain_b, bias_b = norm_backward(stream_b, norm_gain[1], norm_bias[1], d_normed)
    upstream = upstream + d_stream
    d_normed, grad_qkv_a, grad_proj_a = head_backward(
        normed_a, attn_in[0], attn_out[0], stored_a, upstream
    )
    d_stream, gain_a, bias_a = norm_backward(stream_a, norm_gain[0], norm_bias[0], d_normed)
    token_grad = upstream + d_stream
    gain_grads = jnp.stack([gain_a, gain_b, gain_c, gain_d])
    bias_grads = jnp.stack([bias_a, bias_b, bias_c, bias_d])
    grad_attn_in = jnp.stack([grad_qkv_a, grad_qkv_c])
    grad_attn_out = jnp.stack([grad_proj_a, grad_proj_c])
    (
        gain_sum,
        bias_sum,
        attn_in_sum,
        attn_out_sum,
        mlp_in_sum,
        mlp_out_sum,
        expert_in_sum,
        expert_out_sum,
    ) = (
        lax.psum_scatter(
            gain_grads.astype(jnp.bfloat16), "dp", scatter_dimension=1, tiled=True
        ).astype(jnp.float32),
        lax.psum_scatter(
            bias_grads.astype(jnp.bfloat16), "dp", scatter_dimension=1, tiled=True
        ).astype(jnp.float32),
        lax.psum_scatter(
            grad_attn_in.astype(jnp.bfloat16), "dp", scatter_dimension=2, tiled=True
        ).astype(jnp.float32),
        lax.psum_scatter(
            grad_attn_out.astype(jnp.bfloat16), "dp", scatter_dimension=2, tiled=True
        ).astype(jnp.float32),
        lax.psum_scatter(
            grad_mlp_in.astype(jnp.bfloat16), "dp", scatter_dimension=0, tiled=True
        ).astype(jnp.float32),
        lax.psum_scatter(
            grad_mlp_out.astype(jnp.bfloat16), "dp", scatter_dimension=1, tiled=True
        ).astype(jnp.float32),
        lax.psum_scatter(
            grad_ein.astype(jnp.bfloat16), "dp", scatter_dimension=1, tiled=True
        ).astype(jnp.float32),
        lax.psum_scatter(
            grad_eout.astype(jnp.bfloat16), "dp", scatter_dimension=2, tiled=True
        ).astype(jnp.float32),
    )
    return (
        output,
        token_grad,
        gain_sum,
        bias_sum,
        attn_in_sum,
        attn_out_sum,
        mlp_in_sum,
        mlp_out_sum,
        expert_in_sum,
        expert_out_sum,
    )


def solution(mesh):
    placed = (
        P("dp", None),
        P(),
        P(),
        P(None, None, None, "tensor"),
        P(None, "tensor", None),
        P(None, "tensor"),
        P("tensor", None),
        P(None, None, "tensor"),
        P(None, "tensor", None),
        P("dp", None),
        P("dp", None),
        P("dp", None),
        P("dp", None),
    )
    return jax.shard_map(
        local,
        mesh=mesh,
        in_specs=placed,
        out_specs=(
            P("dp", None),
            P("dp", None),
            P(None, "dp"),
            P(None, "dp"),
            P(None, None, "dp", "tensor"),
            P(None, "tensor", "dp"),
            P("dp", "tensor"),
            P("tensor", "dp"),
            P(None, "dp", "tensor"),
            P(None, "tensor", "dp"),
        ),
        check_vma=False,
    )
```

profile of v0, /device:TPU:0, one launch (start us, length us, event | category | flops | bytes accessed | tf_op | source)
XLA Modules:
  0.0 1481.4 jit_solution(15386365710554471401)
XLA Ops:
  10.6 2.6 fusion.128
  18.8 49.2 %all-reduce.20.cloned.1.call-done = f32[394,768]{1,0:T(8,128)} async-done(((f32[394,768]{1,0:T(8,128)}), f32[394,768]{1,0:T(8,128)}) %all-reduce.20.cloned.1.call-update) | async-done | bytes 1210384 | tf_op jit(solution)/shard_map/psum | solution.py:53
  70.5 4.3 multiply_convert_fusion.4
  77.3 42.5 %all-reduce.22.cloned.1.call-done = bf16[394,768]{1,0:T(8,128)(2,1)} async-done(((bf16[394,768]{1,0:T(8,128)(2,1)}), bf16[394,768]{1,0:T(8,128)(2,1)}) %all-reduce.22.cloned.1.call-update) | async-done | bytes 605200 | tf_op jit(solution)/shard_map/psum | solution.py:103
  130.0 40.4 %scatter_fusion = s32[4,169]{1,0:T(4,128)S(1)} fusion(s32[4,169]{1,0:T(4,128)S(1)} %broadcast_in_dim.38, s32[788]{0:T(1024)S(1)} %reshape.270, s32[788]{0:T(1024)S(1)} %reshape.272), kind=kCustom, calls=%fused_computation.4 | custom fusion | bytes 15760 | tf_op jit(solution)/shard_map/scatter | solution.py:131
  170.6 40.4 %scatter_fusion.1 = f32[4,169]{1,0:T(4,128)S(1)} fusion(f32[4,169]{1,0:T(4,128)S(1)} %broadcast_in_dim.46, s32[788]{0:T(1024)S(1)} %reshape.270, f32[788]{0:T(1024)S(1)} %reshape.278), kind=kCustom, calls=%fused_computation.5 | custom fusion | bytes 15760 | tf_op jit(solution)/shard_map/scatter | solution.py:137
  211.1 3.4 gather_fusion.2
  214.5 1.9 fusion.124
  217.4 3.0 gather_fusion
  220.4 4.2 fusion.61
  224.7 5.4 multiply_convert_fusion.1
  230.1 4.3 add_convert_fusion
  236.3 3.8 gather_fusion.3
  240.1 4.4 reshape.267
  244.5 5.5 reduce_sum.281
  250.1 42.1 %all-reduce.26.cloned.1.call-done = bf16[394,768]{1,0:T(8,128)(2,1)} async-done(((bf16[394,768]{1,0:T(8,128)(2,1)}), bf16[394,768]{1,0:T(8,128)(2,1)}) %all-reduce.26.cloned.1.call-update) | async-done | bytes 605200 | tf_op jit(solution)/shard_map/psum | solution.py:175
  292.2 1.7 fusion.27
  302.2 2.8 fusion.18
  305.1 42.1 %all-reduce.28.cloned.1.call-done = bf16[394,768]{1,0:T(8,128)(2,1)} async-done(((bf16[394,768]{1,0:T(8,128)(2,1)}), bf16[394,768]{1,0:T(8,128)(2,1)}) %all-reduce.28.cloned.1.call-update) | async-done | bytes 605200 | tf_op jit(solution)/shard_map/psum | solution.py:92
  354.9 3.3 fusion.133
  358.4 4.0 gather_fusion.1
  362.4 4.1 reshape.247
  366.5 5.6 multiply_reduce_fusion
  372.2 24.9 %all-reduce.30.cloned.1.call-done = bf16[394,768]{1,0:T(8,128)(2,1)} async-done(((bf16[394,768]{1,0:T(8,128)(2,1)}), bf16[394,768]{1,0:T(8,128)(2,1)}) %all-reduce.30.cloned.1.call-update) | async-done | bytes 605200 | tf_op jit(solution)/shard_map/psum | solution.py:118
  403.6 1.7 fusion.48
  409.0 1.8 copy.117
  411.9 1.8 copy.120
  413.7 1.8 stack.77
  417.3 2.8 fusion.19
  420.2 3.4 convolution_convert_fusion.2
  423.6 3.1 convolution_convert_fusion.3
  427.6 2.1 fusion.44
  429.8 1.7 fusion.21
  431.9 1.8 copy.125
  433.7 2.0 fusion.20
  437.2 6.9 copy.124
  444.1 3.4 convolution_convert_fusion
  447.5 3.6 copy.142
  451.2 3.2 copy.145
  454.7 3.0 convolution_convert_fusion.1
  457.7 3.6 copy.140
  461.4 3.2 copy.144
  471.8 158.3 %all-reduce.8 = (bf16[4,768]{1,0:T(4,128)(2,1)S(1)}, bf16[4,768]{1,0:T(4,128)(2,1)S(1)}) all-reduce(bf16[4,768]{1,0:T(4,128)(2,1)S(1)} %pad_maximum_fusion.2, bf16[4,768]{1,0:T(4,128)(2,1)S(1)} %pad_maximum_fusion.3), channel_id=2, replica_groups=mesh['dp'=32,'tensor'=4] {'dp'}, use_global_device_ids=true, to_apply=%region_38.39.clone | all-reduce | flops 6144 | bytes 24576
  631.5 2.4 convert_add_fusion.1
  636.7 155.8 %reduce-scatter.11.cloned.1.call-done = bf16[24,768]{1,0:T(8,128)(2,1)} async-done(((bf16[768,768]{1,0:T(8,128)(2,1)}), bf16[24,768]{1,0:T(8,128)(2,1)}) %reduce-scatter.11.cloned.1.call-update) | async-done | bytes 36880 | tf_op jit(solution)/shard_map/reduce_scatter | solution.py:257
  793.9 325.7 %all-reduce.32.cloned.1.call-done = (bf16[2,3,768,192]{3,0,1,2:T(2,128)(2,1)}, bf16[2,192,768]{1,0,2:T(2,128)(2,1)}) async-done(((bf16[2,3,768,192]{3,0,1,2:T(2,128)(2,1)}, bf16[2,192,768]{1,0,2:T(2,128)(2,1)}), (bf16[2,3,768,192]{3,0,1,2:T(2,128)(2,1)}, bf16[2,192,768]{1,0,2:T(2,128)(2,1)})) %all-reduce.32.cloned.1.call-update) | async-done | bytes 2359312
  1122.6 175.8 %reduce-scatter.17.cloned.1.call-done = bf16[24,3072]{1,0:T(8,128)(2,1)} async-done(((bf16[768,3072]{1,0:T(8,128)(2,1)}), bf16[24,3072]{1,0:T(8,128)(2,1)}) %reduce-scatter.17.cloned.1.call-update) | async-done | bytes 147472
  1300.1 172.2 %reduce-scatter.15.cloned.1.call-done = bf16[24,3072]{1,0:T(8,128)(2,1)} async-done(((bf16[768,3072]{1,0:T(8,128)(2,1)}), bf16[24,3072]{1,0:T(8,128)(2,1)}) %reduce-scatter.15.cloned.1.call-update) | async-done | bytes 147472
  (395 shorter events, 77.3 us)
Async XLA Ops:
  7.2 63.3 %copy-start = (bf16[768,768]{1,0:T(8,128)(2,1)S(1)}, bf16[768,768]{1,0:T(8,128)(2,1)}, u32[]{:S(2)}) copy-start(bf16[768,768]{1,0:T(8,128)(2,1)} %param.18) | copy-start | bytes 3538948
  7.2 60.7 %all-reduce.20.cloned.1.call-start = ((), (), s32[]{:S(2)}) async-start(), calls=%async_computation.4 | async-start | bytes 2457600 | tf_op jit(solution)/shard_map/psum | solution.py:53
  8.6 5.3 copy-start.74
  10.6 3.3 copy-start.81
  10.6 3.3 copy-start.13
  13.8 56.6 %copy-start.62 = (f32[768]{0:T(1024)}, f32[768]{0:T(1024)S(1)}, u32[]{:S(2)}) copy-start(f32[768]{0:T(1024)S(1)} %get-tuple-element.96) | copy-start | bytes 9220
  13.8 56.6 %copy-start.100 = (f32[768]{0:T(1024)}, f32[768]{0:T(1024)S(1)}, u32[]{:S(2)}) copy-start(f32[768]{0:T(1024)S(1)} %get-tuple-element.55) | copy-start | bytes 9220
  13.8 107.5 %copy-start.70 = (f32[768]{0:T(1024)}, f32[768]{0:T(1024)S(1)}, u32[]{:S(2)}) copy-start(f32[768]{0:T(1024)S(1)} %get-tuple-element.94) | copy-start | bytes 9220
  13.9 107.6 %copy-start.98 = (f32[768]{0:T(1024)}, f32[768]{0:T(1024)S(1)}, u32[]{:S(2)}) copy-start(f32[768]{0:T(1024)S(1)} %get-tuple-element.57) | copy-start | bytes 9220
  18.7 101.0 %all-reduce.22.cloned.1.call-start = ((), (), s32[]{:S(2)}) async-start(), calls=%async_computation.5 | async-start | bytes 1228800 | tf_op jit(solution)/shard_map/psum | solution.py:103
  69.4 50.3 %copy-start.4 = (f32[394,768]{1,0:T(8,128)}, f32[394,768]{1,0:T(8,128)S(1)}, u32[]{:S(2)}) copy-start(f32[394,768]{1,0:T(8,128)S(1)} %get-tuple-element.75) | copy-start | bytes 3631108
  69.4 5.4 copy-start.72
  70.5 4.4 copy-start.79
  70.5 5.2 copy-start.103
  77.2 137.2 %all-reduce.24.cloned.1.call-start = ((), (), s32[]{:S(2)}) async-start(), calls=%async_computation.6 | async-start | bytes 2457600 | tf_op jit(solution)/shard_map/psum | solution.py:53
  127.5 164.7 %all-reduce.26.cloned.1.call-start = ((), (), s32[]{:S(2)}) async-start(), calls=%async_computation.7 | async-start | bytes 1228800 | tf_op jit(solution)/shard_map/psum | solution.py:175
  130.0 40.5 %copy-start.23 = (bf16[394,768]{1,0:T(8,128)(2,1)S(1)}, bf16[394,768]{1,0:T(8,128)(2,1)}, u32[]{:S(2)}) copy-start(bf16[394,768]{1,0:T(8,128)(2,1)} %param.25) | copy-start | bytes 1815556
  170.6 40.4 %copy-start.93 = (s32[788]{0:T(1024)S(1)}, s32[788]{0:T(1024)}, u32[]{:S(2)}) copy-start(s32[788]{0:T(1024)} %reshape.248) | copy-start | bytes 9460
  220.4 4.3 copy-start.32
  224.7 5.4 copy-start.28
  224.7 9.7 slice-start
  230.1 4.3 slice-start.1
  244.5 47.7 %copy-start.2 = (f32[394,768]{1,0:T(8,128)S(1)}, f32[394,768]{1,0:T(8,128)}, u32[]{:S(2)}) copy-start(f32[394,768]{1,0:T(8,128)} %copy-done.1) | copy-start | bytes 3631108
  250.1 97.2 %all-reduce.28.cloned.1.call-start = ((), (), s32[]{:S(2)}) async-start(), calls=%async_computation.8 | async-start | bytes 1228800 | tf_op jit(solution)/shard_map/psum | solution.py:92
  302.2 45.0 %copy-start.7 = (f32[394,768]{1,0:T(8,128)S(1)}, f32[394,768]{1,0:T(8,128)}, u32[]{:S(2)}) copy-start(f32[394,768]{1,0:T(8,128)} %copy-done.6) | copy-start | bytes 3631108
  302.2 45.0 %copy-start.71 = (f32[768]{0:T(1024)S(1)}, f32[768]{0:T(1024)}, u32[]{:S(2)}) copy-start(f32[768]{0:T(1024)} %copy-done.70) | copy-start | bytes 9220
  302.2 45.0 %copy-start.77 = (f32[394]{0:T(512)S(1)}, f32[394]{0:T(512)}, u32[]{:S(2)}) copy-start(f32[394]{0:T(512)} %copy-done.76) | copy-start | bytes 4732
  305.0 43.7 %copy-start.88 = (f32[394]{0:T(512)S(1)}, f32[394]{0:T(512)}, u32[]{:S(2)}) copy-start(f32[394]{0:T(512)} %copy-done.87) | copy-start | bytes 4732
  305.0 43.7 %copy-start.90 = (f32[394]{0:T(512)S(1)}, f32[394]{0:T(512)}, u32[]{:S(2)}) copy-start(f32[394]{0:T(512)} %copy-done.89) | copy-start | bytes 4732
  305.0 92.1 %all-reduce.30.cloned.1.call-start = ((), (), s32[]{:S(2)}) async-start(), calls=%async_computation.9 | async-start | bytes 1228800 | tf_op jit(solution)/shard_map/psum | solution.py:118
  354.9 113.1 %all-reduce.34.cloned.1.call-start = ((), (), s32[]{:S(2)}) async-start(), calls=%async_computation.15 | async-start | bytes 2457600 | tf_op jit(solution)/shard_map/psum | solution.py:156
  362.4 4.1 copy-start.39
  366.5 30.6 %copy-start.5 = (f32[394,768]{1,0:T(8,128)S(1)}, f32[394,768]{1,0:T(8,128)}, u32[]{:S(2)}) copy-start(f32[394,768]{1,0:T(8,128)} %copy-done.4) | copy-start | bytes 3631108
  366.5 30.6 %copy-start.63 = (f32[768]{0:T(1024)S(1)}, f32[768]{0:T(1024)}, u32[]{:S(2)}) copy-start(f32[768]{0:T(1024)} %copy-done.62) | copy-start | bytes 9220
  366.5 30.6 %copy-start.73 = (f32[394]{0:T(512)S(1)}, f32[394]{0:T(512)}, u32[]{:S(2)}) copy-start(f32[394]{0:T(512)} %copy-done.72) | copy-start | bytes 4732
  372.2 26.4 %copy-start.86 = (f32[394]{0:T(512)S(1)}, f32[394]{0:T(512)}, u32[]{:S(2)}) copy-start(f32[394]{0:T(512)} %copy-done.85) | copy-start | bytes 4732
  372.2 26.5 %copy-start.80 = (f32[394]{0:T(512)S(1)}, f32[394]{0:T(512)}, u32[]{:S(2)}) copy-start(f32[394]{0:T(512)} %copy-done.79) | copy-start | bytes 4732
  420.1 3.5 copy-start.101
  420.1 215.2 %reduce-scatter.13.cloned.1.call-start = ((), (), s32[]{:S(2)}) async-start(), calls=%async_computation.11 | async-start | bytes 1216512 | tf_op jit(solution)/shard_map/reduce_scatter | solution.py:260
  423.6 368.9 %reduce-scatter.11.cloned.1.call-start = ((), (), s32[]{:S(2)}) async-start(), calls=%async_computation.10 | async-start | bytes 1216512 | tf_op jit(solution)/shard_map/reduce_scatter | solution.py:257
  426.7 3.0 copy-start.8
  426.7 3.0 copy-start.99
  426.7 692.9 %all-reduce.32.cloned.1.call-start = ((), (), s32[]{:S(2)}) async-start(), calls=%async_computation.14 | async-start | bytes 6291456
  444.1 854.3 %reduce-scatter.17.cloned.1.call-start = ((), (), s32[]{:S(2)}) async-start(), calls=%async_computation.13 | async-start | bytes 4866048
  454.4 1018.0 %reduce-scatter.15.cloned.1.call-start = ((), (), s32[]{:S(2)}) async-start(), calls=%async_computation.12 | async-start | bytes 4866048
  464.6 3.1 copy-start.26
  467.9 3.0 copy-start.84
  469.3 162.2 %copy-start.3 = (f32[394,768]{1,0:T(8,128)S(1)}, f32[394,768]{1,0:T(8,128)}, u32[]{:S(2)}) copy-start(f32[394,768]{1,0:T(8,128)} %copy-done.1) | copy-start | bytes 3631108
  (76 other events, 112.8 us)
Sparse Core Ops, SparseCore 0:
  18.8 49.0 all-reduce.19
  77.3 42.3 all-reduce.21
  127.6 46.1 all-reduce.23
  250.2 42.0 all-reduce.25
  305.2 42.0 all-reduce.27
  355.0 42.0 all-reduce.29
  420.2 46.1 all-reduce.33
  468.9 162.7 reduce-scatter.12
  634.1 158.3 reduce-scatter.10
  795.1 324.5 all-reduce.31
  1122.0 176.3 reduce-scatter.16
  1300.6 171.6 reduce-scatter.14
where the time goes:
time: 1490 us; the launch traced here: 1480 us
  waiting for transfers between devices  1030 us (69%)
  local copies, waits for them, and re-layouts  163 us (11%)
  blocking collectives  158 us (11%)
  matrix products  59.7 us (4%)
  other arithmetic  51.8 us (3%)
  between operations  17 us (1%)
    unnamed x15, waiting for transfers between devices  674 us
    unnamed x1, blocking collectives  158 us
    reduce_scatter x1, waiting for transfers between devices, local(): lax.psum_scatter(grad_mlp_in.astype(jnp.bfloat16), 'dp', scatter_dimensio...  156 us
    psum x2, waiting for transfers between devices, head_forward(): mixed_total = lax.psum(partial_sum, 'tensor')  49.2 us
    psum x1, waiting for transfers between devices, dense_forward(): lax.psum(partial_sum.astype(jnp.bfloat16), 'tensor').astype(jnp.float32)  42.5 us
    psum x1, waiting for transfers between devices, head_backward(): lax.psum(d_normed.astype(jnp.bfloat16), 'tensor').astype(jnp.float32)  42.1 us
    psum x1, waiting for transfers between devices, expert_backward(): lax.psum(d_normed.astype(jnp.bfloat16), 'tensor').astype(jnp.float32)  42.1 us
    scatter x1, local copies, waits for them, and re-layouts, expert_tables(): owner_table = jnp.full((expert_count, CAPACITY + 1), row_count, jnp.int32...  40.4 us
  transfers between devices with their start and end apart: 12, of which 9 were waited for; matrix products, arithmetic and copies ran while one was open for 11% of the time, Pallas kernels for 0%

commit v1 on v0

v1 whole, which is shorter than its diff:
```python
import functools
import math

import jax
import jax.numpy as jnp
from jax import lax
from jax.experimental import pallas as pl
from jax.experimental.pallas import tpu as pltpu
from jax.sharding import PartitionSpec as P

HEAD_DIM = 64
SEQ = 197
PAD = 208
CAPACITY = 168
NORM_EPSILON = 1e-06
MESH = pl.DeviceIdType.MESH
F32 = jnp.float32
BF16 = jnp.bfloat16


def tensor_sum_kernel(x_ref, o_ref, from_core, mine, from_chip, send, recv):
    dp = lax.axis_index("dp")
    t = lax.axis_index("tensor")
    core = lax.rem(t, 2)
    other = (dp, t + 1 - 2 * core)
    far = (dp, lax.rem(t + 2, 4))
    barrier = pltpu.get_barrier_semaphore()
    for device in (other, far):
        pl.semaphore_signal(barrier, inc=1, device_id=device, device_id_type=MESH)
    pl.semaphore_wait(barrier, 2)
    count = x_ref.shape[0] // 2

    def remote(source, target, slot, device):
        return pltpu.make_async_remote_copy(
            src_ref=source,
            dst_ref=target,
            send_sem=send.at[slot],
            recv_sem=recv.at[slot],
            device_id=device,
            device_id_type=MESH,
        )

    first = remote(x_ref.at[pl.ds((1 - core) * count, count)], from_core, 0, other)
    first.start()
    first.wait()
    for i in range(count):
        mine[i] = (x_ref[core * count + i].astype(F32) + from_core[i].astype(F32)).astype(BF16)
    second = remote(mine, from_chip, 1, far)
    second.start()
    second.wait()
    for i in range(count):
        o_ref[core * count + i] = mine[i].astype(F32) + from_chip[i].astype(F32)
    half = o_ref.at[pl.ds(core * count, count)]
    third = remote(half, half, 2, other)
    third.start()
    third.wait()


def tensor_sum(parts, collective_id):
    rows, width = parts[0].shape
    stacked = jnp.stack(
        [
            jnp.pad(p.astype(BF16)[i * SEQ : (i + 1) * SEQ], ((0, PAD - SEQ), (0, 0)))
            for i in range(2)
            for p in parts
        ]
    )
    count = len(parts)
    total = pl.pallas_call(
        tensor_sum_kernel,
        out_shape=jax.ShapeDtypeStruct(stacked.shape, F32),
        in_specs=[pl.BlockSpec(memory_space=pltpu.VMEM)],
        out_specs=pl.BlockSpec(memory_space=pltpu.VMEM),
        scratch_shapes=[
            pltpu.VMEM((count, PAD, width), BF16),
            pltpu.VMEM((count, PAD, width), BF16),
            pltpu.VMEM((count, PAD, width), BF16),
            pltpu.SemaphoreType.DMA((3,)),
            pltpu.SemaphoreType.DMA((3,)),
        ],
        compiler_params=pltpu.CompilerParams(
            collective_id=collective_id, has_side_effects=True, vmem_limit_bytes=40 << 20
        ),
        name="tensor_sum",
    )(stacked)
    return [
        jnp.concatenate([total[i, :SEQ], total[count + i, :SEQ]], axis=0) for i in range(count)
    ]


def grid_device(y, z, x):
    return (lax.rem(y + 8, 4) * 4 + lax.rem(z + 8, 4)) * 2 + x


def image_sum_kernel(orders, *refs):
    n = len(orders)
    g_refs, o_refs = refs[:n], refs[n : 2 * n]
    owns, gots, sums, gots2, totals, outs3, gots3 = (
        refs[2 * n + k * n : 2 * n + (k + 1) * n] for k in range(7)
    )
    send, recv, local_sem = refs[9 * n :]
    dp = lax.axis_index("dp")
    t = lax.axis_index("tensor")
    y, z, x = dp // 8, lax.rem(dp // 2, 4), lax.rem(dp, 2)

    barrier = pltpu.get_barrier_semaphore()
    for k in (1, 2, 3):
        for device in (grid_device(y + k, z, x), grid_device(y, z + k, x)):
            pl.semaphore_signal(barrier, inc=1, device_id=(device, t), device_id_type=MESH)
    pl.semaphore_signal(barrier, inc=1, device_id=(grid_device(y, z, 1 - x), t), device_id_type=MESH)
    pl.semaphore_wait(barrier, 7)

    def remote(source, target, slot, device):
        return pltpu.make_async_remote_copy(
            src_ref=source,
            dst_ref=target,
            send_sem=send.at[slot],
            recv_sem=recv.at[slot],
            device_id=(device, t),
            device_id_type=MESH,
        )

    first, locals_ = [], []
    for i, order in enumerate(orders):
        copies = []
        for k in (2, 1, 3):
            if order == "y":
                source, device = g_refs[i].at[:, lax.rem(y + k, 4)], grid_device(y + k, z, x)
            else:
                source, device = g_refs[i].at[:, :, lax.rem(z + k, 4)], grid_device(y, z + k, x)
            copies.append(remote(source, gots[i].at[k - 1], i * 7 + k - 1, device))
            copies[-1].start()
        first.append(copies)
        source = g_refs[i].at[:, y] if order == "y" else g_refs[i].at[:, :, z]
        locals_.append(pltpu.make_async_copy(source, owns[i], local_sem.at[i]))
        locals_[-1].start()
    second = []
    for i, order in enumerate(orders):
        locals_[i].wait()
        for copy in first[i]:
            copy.wait()

        def add(m, carry, i=i):
            for b in range(4):
                acc = owns[i][m, b].astype(F32)
                for k in range(3):
                    acc = acc + gots[i][k, m, b].astype(F32)
                sums[i][m, b] = acc.astype(BF16)
            return carry

        lax.fori_loop(0, owns[i].shape[0], add, 0)
        copies = []
        for k in (2, 1, 3):
            if order == "y":
                index, device = lax.rem(z + k, 4), grid_device(y, z + k, x)
            else:
                index, device = lax.rem(y + k, 4), grid_device(y + k, z, x)
            copies.append(remote(sums[i].at[:, index], gots2[i].at[k - 1], i * 7 + 2 + k, device))
            copies[-1].start()
        second.append(copies)
    third = []
    for i, order in enumerate(orders):
        for copy in second[i]:
            copy.wait()
        own = z if order == "y" else y

        def add(m, carry, i=i, own=own):
            acc = sums[i][m, own].astype(F32)
            for k in range(3):
                acc = acc + gots2[i][k, m].astype(F32)
            totals[i][m] = acc
            return carry

        count = owns[i].shape[0]
        lax.fori_loop(0, count, add, 0)
        other = pl.ds(pl.multiple_of((1 - x) * 24, 8), 24)
        if count > 1:
            for m in range(0, count, 2):
                pair = jnp.concatenate([totals[i][m, other], totals[i][m + 1, other]], axis=0)
                outs3[i][m // 2] = pair.astype(BF16)
        else:
            alone = totals[i][0, other]
            outs3[i][0] = jnp.concatenate([alone, alone], axis=0).astype(BF16)
        third.append(remote(outs3[i], gots3[i], i * 7 + 6, grid_device(y, z, 1 - x)))
        third[-1].start()
    for i in range(n):
        third[i].wait()
        mine = pl.ds(pl.multiple_of(x * 24, 8), 24)
        for m in range(owns[i].shape[0]):
            theirs = gots3[i][m // 2].astype(F32)
            o_refs[i][m] = totals[i][m, mine] + theirs[24 * (m % 2) : 24 * (m % 2) + 24]


def image_sum(groups, orders, collective_id):
    n = len(groups)
    shaped = [g.reshape(g.shape[0], 4, 4, 48, g.shape[2]) for g in groups]
    dims = [(g.shape[0], g.shape[2]) for g in groups]
    scratch = (
        [pltpu.VMEM((c, 4, 48, w), BF16) for c, w in dims]
        + [pltpu.VMEM((3, c, 4, 48, w), BF16) for c, w in dims]
        + [pltpu.VMEM((c, 4, 48, w), BF16) for c, w in dims]
        + [pltpu.VMEM((3, c, 48, w), BF16) for c, w in dims]
        + [pltpu.VMEM((c, 48, w), F32) for c, w in dims]
        + [pltpu.VMEM(((c + 1) // 2, 48, w), BF16) for c, w in dims]
        + [pltpu.VMEM(((c + 1) // 2, 48, w), BF16) for c, w in dims]
        + [
            pltpu.SemaphoreType.DMA((7 * n,)),
            pltpu.SemaphoreType.DMA((7 * n,)),
            pltpu.SemaphoreType.DMA((n,)),
        ]
    )
    return pl.pallas_call(
        functools.partial(image_sum_kernel, orders),
        out_shape=[jax.ShapeDtypeStruct((c, 24, w), F32) for c, w in dims],
        in_specs=[pl.BlockSpec(memory_space=pl.ANY)] * n,
        out_specs=[pl.BlockSpec(memory_space=pltpu.VMEM)] * n,
        scratch_shapes=scratch,
        compiler_params=pltpu.CompilerParams(
            collective_id=collective_id, has_side_effects=True, vmem_limit_bytes=50 << 20
        ),
        name="image_sum",
    )(*shaped)


def layer_norm(values, gain_row, bias_row):
    center = values - jnp.mean(values, axis=-1, keepdims=True)
    spread = jnp.mean(center * center, axis=-1, keepdims=True)
    return center * lax.rsqrt(spread + NORM_EPSILON) * gain_row + bias_row


def norm_backward(values, gain_row, bias_row, upstream):
    unused, pullback = jax.vjp(layer_norm, values, gain_row, bias_row)
    return pullback(upstream)


def gelu_exact(values):
    return jax.nn.gelu(values, approximate=False)


def gelu_back(hidden, upstream):
    unused, pullback = jax.vjp(gelu_exact, hidden)
    return pullback(upstream)[0]


def head_scores(shaped):
    scaling = 1.0 / math.sqrt(HEAD_DIM)
    return jnp.einsum("bqhd,bkhd->bhqk", shaped[0], shaped[1], preferred_element_type=F32) * scaling


def head_forward(normed, weight_in, weight_out):
    projected = jnp.einsum("nd,jde->jne", normed, weight_in, preferred_element_type=F32).astype(BF16)
    images = normed.shape[0] // SEQ
    local_heads = weight_in.shape[2] // HEAD_DIM
    shaped = projected.reshape(3, images, SEQ, local_heads, HEAD_DIM)
    scores = head_scores(shaped)
    highest = jnp.max(scores, axis=-1, keepdims=True)
    log_total = highest + jnp.log(jnp.sum(jnp.exp(scores - highest), axis=-1, keepdims=True))
    weights = jnp.exp(scores - log_total).astype(BF16)
    mixture = jnp.einsum("bhqk,bkhd->bqhd", weights, shaped[2], preferred_element_type=F32)
    mixture = mixture.astype(BF16).reshape(normed.shape[0], weight_in.shape[2])
    partial_sum = jnp.dot(mixture, weight_out, preferred_element_type=F32)
    return (partial_sum, (shaped, log_total, mixture))


def head_backward(normed, weight_in, weight_out, stored, upstream):
    shaped, log_total, mixture = stored
    scaling = 1.0 / math.sqrt(HEAD_DIM)
    upstream_low = upstream.astype(BF16)
    grad_out = jnp.einsum("nd,ne->de", upstream_low, mixture, preferred_element_type=F32)
    d_mixture = jnp.einsum("nd,ed->ne", upstream_low, weight_out, preferred_element_type=F32).astype(BF16)
    d_mixture = d_mixture.reshape(shaped.shape[1:])
    probability = jnp.exp(head_scores(shaped) - log_total)
    d_weights = jnp.einsum("bqhd,bkhd->bhqk", d_mixture, shaped[2], preferred_element_type=F32)
    centered = d_weights - jnp.sum(probability * d_weights, axis=-1, keepdims=True)
    d_scores = (probability * centered).astype(BF16)
    d_query = (
        jnp.einsum("bhqk,bkhd->bqhd", d_scores, shaped[1], preferred_element_type=F32) * scaling
    ).astype(BF16)
    d_keys = (
        jnp.einsum("bhqk,bqhd->bkhd", d_scores, shaped[0], preferred_element_type=F32) * scaling
    ).astype(BF16)
    d_values = jnp.einsum(
        "bhqk,bqhd->bkhd", probability.astype(BF16), d_mixture, preferred_element_type=F32
    ).astype(BF16)
    flat = [v.reshape(normed.shape[0], weight_in.shape[2]) for v in (d_query, d_keys, d_values)]
    d_projected = jnp.concatenate(flat, axis=1)
    grad_in = jnp.einsum("nd,ne->de", normed, d_projected, preferred_element_type=F32)
    d_normed = jnp.einsum("jne,jde->nd", jnp.stack(flat), weight_in, preferred_element_type=F32)
    grads = jnp.concatenate([grad_in.astype(BF16), grad_out.astype(BF16)], axis=1)
    return (d_normed, grads)


def dense_forward(normed, weight_in, weight_out):
    hidden = jnp.dot(normed, weight_in, preferred_element_type=F32)
    active = gelu_exact(hidden).astype(BF16)
    return (jnp.dot(active, weight_out, preferred_element_type=F32), (hidden, active))


def dense_backward(normed, weight_in, weight_out, stored, upstream):
    hidden, active = stored
    upstream_low = upstream.astype(BF16)
    grad_out = jnp.einsum("nd,nf->df", upstream_low, active, preferred_element_type=F32)
    d_active = jnp.einsum("nd,fd->nf", upstream_low, weight_out, preferred_element_type=F32)
    d_hidden = gelu_back(hidden, d_active).astype(BF16)
    grad_in = jnp.einsum("nd,nf->df", normed, d_hidden, preferred_element_type=F32)
    d_normed = jnp.einsum("nf,df->nd", d_hidden, weight_in, preferred_element_type=F32)
    return (d_normed, grad_in.astype(BF16), grad_out.astype(BF16))


def experts(normed, weight_in, weight_out, routes, slot_index, gate_weights, cotangent):
    count = weight_in.shape[0]
    width = normed.shape[1]
    flat = jnp.where(slot_index < CAPACITY, routes * CAPACITY + slot_index, -1)
    slots = lax.broadcasted_iota(jnp.int32, (count * CAPACITY, normed.shape[0]), 0)
    hits = [slots == flat[:, k][None, :] for k in range(2)]
    pick = jnp.logical_or(*hits).astype(BF16)
    gate = sum(
        jnp.sum(jnp.where(hits[k], gate_weights[:, k][None, :], 0.0), axis=1, keepdims=True)
        for k in range(2)
    )
    shape = (count, CAPACITY, width)
    buffer = jnp.dot(pick, normed, preferred_element_type=F32).astype(BF16).reshape(shape)
    d_rows = jnp.dot(pick, cotangent, preferred_element_type=F32) * gate
    d_rows = d_rows.astype(BF16).reshape(shape)
    hidden = jnp.einsum("ecd,edf->ecf", buffer, weight_in, preferred_element_type=F32)
    active = gelu_exact(hidden).astype(BF16)
    rows = jnp.einsum("ecf,efd->ecd", active, weight_out, preferred_element_type=F32)
    weighted = (rows.reshape(-1, width) * gate).astype(BF16)
    forward = jnp.einsum("sn,sd->nd", pick, weighted, preferred_element_type=F32)
    grad_out = jnp.einsum("ecd,ecf->edf", d_rows, active, preferred_element_type=F32)
    d_active = jnp.einsum("ecd,efd->ecf", d_rows, weight_out, preferred_element_type=F32)
    d_hidden = gelu_back(hidden, d_active).astype(BF16)
    grad_in = jnp.einsum("ecd,ecf->edf", buffer, d_hidden, preferred_element_type=F32)
    d_buffer = jnp.einsum("ecf,edf->ecd", d_hidden, weight_in, preferred_element_type=F32)
    d_normed = jnp.einsum(
        "sn,sd->nd", pick, d_buffer.reshape(-1, width).astype(BF16), preferred_element_type=F32
    )
    return (forward, d_normed, grad_in.astype(BF16), grad_out.astype(BF16))


def local(
    tokens,
    norm_gain,
    norm_bias,
    attn_in,
    attn_out,
    mlp_in,
    mlp_out,
    expert_in,
    expert_out,
    routes,
    slot_index,
    gate_weights,
    cotangent,
):
    stream_a = tokens.astype(F32)
    normed_a = layer_norm(stream_a, norm_gain[0], norm_bias[0]).astype(BF16)
    part, stored_a = head_forward(normed_a, attn_in[0], attn_out[0])
    stream_b = stream_a + tensor_sum([part], 1)[0]
    normed_b = layer_norm(stream_b, norm_gain[1], norm_bias[1]).astype(BF16)
    part, stored_b = dense_forward(normed_b, mlp_in, mlp_out)
    stream_c = stream_b + tensor_sum([part], 1)[0]
    normed_c = layer_norm(stream_c, norm_gain[2], norm_bias[2]).astype(BF16)
    part, stored_c = head_forward(normed_c, attn_in[1], attn_out[1])
    stream_d = stream_c + tensor_sum([part], 1)[0]
    normed_d = layer_norm(stream_d, norm_gain[3], norm_bias[3]).astype(BF16)
    part, d_part, grad_ein, grad_eout = experts(
        normed_d, expert_in, expert_out, routes, slot_index, gate_weights, cotangent
    )
    mixed_d, d_normed = tensor_sum([part, d_part], 2)
    output = stream_d + mixed_d
    upstream = cotangent.astype(F32)
    d_stream, gain_d, bias_d = norm_backward(stream_d, norm_gain[3], norm_bias[3], d_normed)
    upstream = upstream + d_stream
    d_part, grads_c = head_backward(normed_c, attn_in[1], attn_out[1], stored_c, upstream)
    d_normed = tensor_sum([d_part], 1)[0]
    d_stream, gain_c, bias_c = norm_backward(stream_c, norm_gain[2], norm_bias[2], d_normed)
    upstream = upstream + d_stream
    d_part, grad_min, grad_mout = dense_backward(normed_b, mlp_in, mlp_out, stored_b, upstream)
    d_normed = tensor_sum([d_part], 1)[0]
    d_stream, gain_b, bias_b = norm_backward(stream_b, norm_gain[1], norm_bias[1], d_normed)
    upstream = upstream + d_stream
    d_part, grads_a = head_backward(normed_a, attn_in[0], attn_out[0], stored_a, upstream)
    d_normed = tensor_sum([d_part], 1)[0]
    d_stream, gain_a, bias_a = norm_backward(stream_a, norm_gain[0], norm_bias[0], d_normed)
    token_grad = upstream + d_stream
    norms = jnp.stack([gain_a, gain_b, gain_c, gain_d, bias_a, bias_b, bias_c, bias_d], axis=1)
    norms = jnp.pad(norms, ((0, 0), (0, 120))).astype(BF16)[None]
    ein, eout, dense, heads, norms = image_sum(
        [
            grad_ein,
            grad_eout,
            jnp.stack([grad_min, grad_mout]),
            jnp.stack([grads_a, grads_c]),
            norms,
        ],
        ("y", "z", "y", "z", "y"),
        3,
    )
    head_width = attn_out.shape[1]
    attn_in_sum = jnp.stack(
        [heads[:, :, c * head_width : (c + 1) * head_width] for c in range(3)], axis=1
    )
    return (
        output,
        token_grad,
        norms[0, :, :4].T,
        norms[0, :, 4:8].T,
        attn_in_sum,
        jnp.swapaxes(heads[:, :, 3 * head_width :], 1, 2),
        dense[0],
        dense[1].T,
        ein,
        jnp.swapaxes(eout, 1, 2),
    )


def solution(mesh):
    placed = (
        P("dp", None),
        P(),
        P(),
        P(None, None, None, "tensor"),
        P(None, "tensor", None),
        P(None, "tensor"),
        P("tensor", None),
        P(None, None, "tensor"),
        P(None, "tensor", None),
        P("dp", None),
        P("dp", None),
        P("dp", None),
        P("dp", None),
    )
    return jax.shard_map(
        local,
        mesh=mesh,
        in_specs=placed,
        out_specs=(
            P("dp", None),
            P("dp", None),
            P(None, "dp"),
            P(None, "dp"),
            P(None, None, "dp", "tensor"),
            P(None, "tensor", "dp"),
            P("dp", "tensor"),
            P("tensor", "dp"),
            P(None, "dp", "tensor"),
            P(None, "tensor", "dp"),
        ),
        check_vma=False,
    )
```

time: 1490 us -> 380 us (0.26)
  waiting for transfers between devices: 1030 us -> 0 us
  Pallas kernels: 0 us -> 222 us
  blocking collectives: 158 us -> 0 us
  local copies, waits for them, and re-layouts: 163 us -> 65.5 us
  other arithmetic: 51.8 us -> 30.4 us
    unnamed x15 -> x0, waiting for transfers between devices: 674 us -> none
    pallas_call x0 -> x8, Pallas kernels: none -> 222 us  [the longest x7 112 us: tensor_sum(): pl.pallas_call(tensor_sum_kernel, out_shape=jax.ShapeDtypeStruct(stacked....]
    psum x7 -> x0, waiting for transfers between devices: 201 us -> none  [the longest x2 49.2 us: head_forward(): mixed_total = lax.psum(partial_sum, 'tensor')]
    unnamed x1 -> x0, blocking collectives: 158 us -> none
    reduce_scatter x2 -> x0, waiting for transfers between devices: 156 us -> none  [the longest x1 156 us: local(): lax.psum_scatter(grad_mlp_in.astype(jnp.bfloat16), 'dp', scatter_dimensio...]
    scatter x2 -> x0, local copies, waits for them, and re-layouts: 80.8 us -> none  [the longest x1 40.4 us: expert_tables(): owner_table = jnp.full((expert_count, CAPACITY + 1), row_count, jnp.int32...]
    gather x6 -> x0, local copies, waits for them, and re-layouts: 22.6 us -> none  [the longest x2 8.2 us: expert_backward(): d_normed = jnp.sum(flat_back[flat_index], axis=1)]
    unnamed x237 -> x172, local copies, waits for them, and re-layouts: 33.5 us -> 15.8 us
  transfers between devices with their start and end apart: 12 -> 0, of which waited for: 9 -> 0; matrix products, arithmetic and copies ran while one was open for 11% -> 0% of each run, Pallas kernels for 0% -> 0%
where the time goes in v1:
time: 380 us; the launch traced here: 374 us
  Pallas kernels  222 us (58%)
  local copies, waits for them, and re-layouts  65.5 us (17%)
  matrix products  52.7 us (14%)
  other arithmetic  30.4 us (8%)
    pallas_call x7, Pallas kernels, tensor_sum(): pl.pallas_call(tensor_sum_kernel, out_shape=jax.ShapeDtypeStruct(stacked....  112 us
    pallas_call x1, Pallas kernels, image_sum(): pl.pallas_call(functools.partial(image_sum_kernel, orders), out_shape=[ja...  110 us
    unnamed x172, local copies, waits for them, and re-layouts  15.8 us
    another operation x6, local copies, waits for them, and re-layouts, head_backward(): jnp.stack(flat)  8.67 us
    reshape x6, local copies, waits for them, and re-layouts, head_backward(): v.reshape(normed.shape[0], weight_in.shape[2])  8.64 us

profile of v1, /device:TPU:0, one launch (start us, length us, event | category | flops | bytes accessed | tf_op | source)
XLA Modules:
  0.0 373.7 jit_solution(12720023297019008775)
XLA Ops:
  0.7 1.4 convert_reduce_fusion
  2.1 1.4 fusion.18
  4.1 1.9 multiply_convert_fusion
  12.1 1.4 convolution_convert_fusion.13
  13.8 14.8 %tensor_sum.7 = f32[2,208,768]{2,1,0:T(8,128)S(1)} custom-call(bf16[2,208,768]{2,1,0:T(8,128)(2,1)S(1)} %pad_maximum_fusion.9.x_ref), custom_call_target="tpu_custom_call" | custom-call | tf_op jit(solution)/shard_map/tensor_sum/pallas_call | solution.py:69
  29.3 4.8 %multiply_convert_fusion.4 = (bf16[394,768]{1,0:T(8,128)(2,1)S(1)}, f32[394,768]{1,0:T(8,128)}, f32[394,768]{1,0:T(8,128)}) fusion(bf16[768,768]{1,0:T(8,128)(2,1)S(1)} %copy-done, f32[394,768]{1,0:T(8,128)S(1)} %get-tuple-element.91, f32[768]{0:T(1024)S(1)} %get-tuple-element.73, f32[768]{0:T(1024)S(1)} %get-tuple-element.143, f32[394]{0:T(512)S(1)} %fusion.120, ...), kind=kOutput, calls=%fused_computation.100 | convolution fusion | flops 485962752 | bytes 5425232 | tf_op jit(solution)/shard_map/dot_general | solution.py:294
  35.2 14.8 %tensor_sum.8 = f32[2,208,768]{2,1,0:T(8,128)S(1)} custom-call(bf16[2,208,768]{2,1,0:T(8,128)(2,1)S(1)} %pad_maximum_fusion.10.x_ref), custom_call_target="tpu_custom_call" | custom-call | tf_op jit(solution)/shard_map/tensor_sum/pallas_call | solution.py:69
  50.8 1.3 copy-done.44
  54.2 1.3 fusion.150
  58.0 1.3 convolution_convert_fusion.11
  59.7 14.8 %tensor_sum.9 = f32[2,208,768]{2,1,0:T(8,128)S(1)} custom-call(bf16[2,208,768]{2,1,0:T(8,128)(2,1)S(1)} %pad_maximum_fusion.11.x_ref), custom_call_target="tpu_custom_call" | custom-call | tf_op jit(solution)/shard_map/tensor_sum/pallas_call | solution.py:69
  74.6 1.2 copy-done.10
  76.4 1.1 convolution_convert_fusion.5
  77.5 1.5 fusion.69
  79.1 4.8 %multiply_convert_fusion.1 = (bf16[4,168,768]{2,1,0:T(8,128)(2,1)S(1)}, f32[4,168,768]{2,1,0:T(8,128)S(1)}) fusion(f32[4,168,768]{2,1,0:T(8,128)S(1)} %get-tuple-element.136, u8[168,768]{1,0:T(8,128)(4,1)S(1)} %get-tuple-element.59, u8[168,768]{1,0:T(8,128)(4,1)S(1)} %get-tuple-element.58), kind=kLoop, calls=%fused_computation.15 | loop fusion | flops 36126720 | bytes 5419008 | tf_op jit(solution)/shard_map/convert_element_type | solution.py:326
  84.0 1.9 add_convert_fusion
  85.8 1.7 convolution_convert_fusion.4
  90.9 23.2 %tensor_sum.10 = f32[4,208,768]{2,1,0:T(8,128)S(1)} custom-call(bf16[4,208,768]{2,1,0:T(8,128)(2,1)S(1)} %pad_maximum_fusion.2.x_ref), custom_call_target="tpu_custom_call" | custom-call | tf_op jit(solution)/shard_map/tensor_sum/pallas_call | solution.py:69
  115.5 1.6 fusion.137
  122.6 1.8 reshape.319
  124.4 1.8 stack_reshape.20
  131.8 3.0 fusion.13
  135.8 1.1 pad_maximum_fusion.8
  136.9 2.6 copy.135
  141.7 14.8 %tensor_sum.11 = f32[2,208,768]{2,1,0:T(8,128)S(1)} custom-call(bf16[2,208,768]{2,1,0:T(8,128)(2,1)S(1)} %pad_maximum_fusion.12.x_ref), custom_call_target="tpu_custom_call" | custom-call | tf_op jit(solution)/shard_map/tensor_sum/pallas_call | solution.py:69
  166.8 14.8 %tensor_sum.12 = f32[2,208,768]{2,1,0:T(8,128)S(1)} custom-call(bf16[2,208,768]{2,1,0:T(8,128)(2,1)S(1)} %pad_maximum_fusion.13.x_ref), custom_call_target="tpu_custom_call" | custom-call | tf_op jit(solution)/shard_map/tensor_sum/pallas_call | solution.py:69
  186.7 1.8 reshape.311
  188.4 1.7 fusion.34
  191.1 1.8 reshape.316
  192.8 1.7 stack_reshape.23
  194.6 2.0 multiply_reduce_fusion.3
  199.8 1.8 reshape.315
  201.6 1.8 stack_reshape.22
  203.3 1.7 reshape.314
  205.1 1.8 stack_reshape.21
  206.9 3.1 fusion.14
  212.1 2.6 copy.131
  214.7 3.3 pad_maximum_fusion.1.refs_3_
  218.3 14.8 %tensor_sum.13 = f32[2,208,768]{2,1,0:T(8,128)S(1)} custom-call(bf16[2,208,768]{2,1,0:T(8,128)(2,1)S(1)} %pad_maximum_fusion.14.x_ref), custom_call_target="tpu_custom_call" | custom-call | tf_op jit(solution)/shard_map/tensor_sum/pallas_call | solution.py:69
  234.8 1.3 fusion.17
  236.7 1.4 stack.164
  238.8 3.3 add_add_fusion.4
  242.1 1.5 copy.148
  244.6 5.3 %convolution_convert_fusion = bf16[4,768,768]{2,1,0:T(8,128)(2,1)} fusion(bf16[4,168,768]{2,1,0:T(8,128)(2,1)} %bitcast.250, bf16[4,168,768]{2,1,0:T(8,128)(2,1)} %copy-done.22), kind=kOutput, calls=%fused_computation.1 | convolution fusion | flops 795082752 | bytes 6782976 | tf_op jit(solution)/shard_map/ecd,ecf->edf/dot_general | solution.py:330
  249.9 3.7 convolution_convert_fusion.1
  253.6 110.1 %image_sum.1 = (f32[4,24,768]{2,1,0:T(8,128)S(1)}, f32[4,24,768]{2,1,0:T(8,128)S(1)}, f32[2,24,768]{2,1,0:T(8,128)S(1)}, f32[2,24,768]{2,1,0:T(8,128)S(1)}, f32[1,24,128]{2,1,0:T(8,128)S(1)}) custom-call(bf16[4,4,4,48,768]{4,3,2,1,0:T(8,128)(2,1)} %bitcast.239, bf16[4,4,4,48,768]{4,3,2,1,0:T(8,128)(2,1)} %bitcast.238, ...), custom_call_target="tpu_custom_call" | custom-call | tf_op jit(solution)/shard_map/image_sum/pallas_call | solution.py:212
  367.8 1.6 slice_bitcast_fusion.16
  369.4 1.7 slice_bitcast_fusion.18
  (322 shorter events, 64.9 us)
Async XLA Ops:
  0.6 28.7 %copy-start = (bf16[768,768]{1,0:T(8,128)(2,1)S(1)}, bf16[768,768]{1,0:T(8,128)(2,1)}, u32[]{:S(2)}) copy-start(bf16[768,768]{1,0:T(8,128)(2,1)} %param.18) | copy-start | bytes 3538948
  0.7 3.4 copy-start.25
  0.7 2.9 copy-start.73
  0.7 2.8 copy-start.71
  0.7 2.8 copy-start.72
  0.7 3.2 copy-start.67
  0.7 3.2 copy-start.68
  3.5 2.6 copy-start.63
  3.5 3.5 copy-start.59
  4.0 3.0 copy-start.69
  4.0 160.5 %copy-start.53 = (f32[768]{0:T(1024)}, f32[768]{0:T(1024)S(1)}, u32[]{:S(2)}) copy-start(f32[768]{0:T(1024)S(1)} %get-tuple-element.143) | copy-start | bytes 9220
  4.1 2.0 copy-start.27
  11.7 1.9 copy-start.57
  29.0 21.2 %copy-start.12 = (f32[394,768]{1,0:T(8,128)}, f32[394,768]{1,0:T(8,128)S(1)}, u32[]{:S(2)}) copy-start(f32[394,768]{1,0:T(8,128)S(1)} %get-tuple-element.91) | copy-start | bytes 3631108
  29.0 135.5 %copy-start.55 = (f32[394]{0:T(512)}, f32[394]{0:T(512)S(1)}, u32[]{:S(2)}) copy-start(f32[394]{0:T(512)S(1)} %broadcast_multiply_fusion.2) | copy-start | bytes 4732
  29.3 4.8 %copy-start.65 = (f32[394]{0:T(512)}, f32[394]{0:T(512)S(1)}, u32[]{:S(2)}) copy-start(f32[394]{0:T(512)S(1)} %multiply_reduce_fusion.10) | copy-start | bytes 4732
  29.3 135.2 %copy-start.61 = (f32[394]{0:T(512)}, f32[394]{0:T(512)S(1)}, u32[]{:S(2)}) copy-start(f32[394]{0:T(512)S(1)} %fusion.120) | copy-start | bytes 4732
  29.3 4.8 %copy-start.74 = (bf16[768,768]{1,0:T(8,128)(2,1)S(1)}, bf16[768,768]{1,0:T(8,128)(2,1)}, u32[]{:S(2)}) copy-start(bf16[768,768]{1,0:T(8,128)(2,1)} %param.19) | copy-start | bytes 3538948
  50.4 2.4 copy-start.9
  53.2 2.5 copy-start.32
  74.5 3.0 slice-start
  76.3 7.6 %slice-start.2 = ((s8[4718592]{0:T(1024)(128)(4,1)}), s8[4194304]{0:T(1024)(128)(4,1)S(1)}, s32[]{:S(2)}) async-start(s8[4718592]{0:T(1024)(128)(4,1)} %bitcast.242), calls=%async_computation.2 | async-start | bytes 8388608
  77.5 6.4 %slice-start.3 = ((s8[4718592]{0:T(1024)(128)(4,1)}), s8[524288]{0:T(1024)(128)(4,1)S(1)}, s32[]{:S(2)}) async-start(s8[4718592]{0:T(1024)(128)(4,1)} %bitcast.242), calls=%async_computation.3 | async-start | bytes 1048576
  79.1 4.9 %copy-start.41 = (bf16[672,768]{1,0:T(8,128)(2,1)S(1)}, bf16[672,768]{1,0:T(8,128)(2,1)}, u32[]{:S(2)}) copy-start(bf16[672,768]{1,0:T(8,128)(2,1)} %multiply_convert_fusion) | copy-start | bytes 3096580
  83.9 4.6 %copy-start.22 = (bf16[4,168,768]{2,1,0:T(8,128)(2,1)}, bf16[4,168,768]{2,1,0:T(8,128)(2,1)S(1)}, u32[]{:S(2)}) copy-start(bf16[4,168,768]{2,1,0:T(8,128)(2,1)S(1)} %get-tuple-element.82) | copy-start | bytes 3096580
  128.1 3.7 copy-start.48
  131.8 3.0 copy-start.11
  131.8 3.0 copy-start.46
  131.8 3.0 copy-start.49
  131.8 3.0 copy-start.51
  159.2 2.0 copy-start.79
  183.8 1.8 copy-start.17
  183.8 1.8 copy-start.38
  194.6 2.0 copy-start.8
  206.8 3.1 copy-start.15
  206.9 3.1 copy-start.47
  206.9 3.1 copy-start.50
  206.9 3.1 copy-start.52
  206.9 3.1 copy-start.60
  206.9 3.1 copy-start.70
  214.7 3.3 copy-start.45
  214.7 3.4 copy-start.58
  233.3 2.8 copy-start.20
  233.3 2.8 copy-start.21
  244.6 5.3 %copy-start.24 = (bf16[4,168,768]{2,1,0:T(8,128)(2,1)S(1)}, bf16[4,168,768]{2,1,0:T(8,128)(2,1)}, u32[]{:S(2)}) copy-start(bf16[4,168,768]{2,1,0:T(8,128)(2,1)} %copy-done.23) | copy-start | bytes 3096580
  244.6 5.3 %copy-start.43 = (bf16[672,768]{1,0:T(8,128)(2,1)S(1)}, bf16[672,768]{1,0:T(8,128)(2,1)}, u32[]{:S(2)}) copy-start(bf16[672,768]{1,0:T(8,128)(2,1)} %copy-done.42) | copy-start | bytes 3096580
  366.5 5.3 %copy-start.4 = (f32[4,24,768]{2,1,0:T(8,128)S(1)}, f32[4,24,768]{2,1,0:T(8,128)}, u32[]{:S(2)}) copy-start(f32[4,24,768]{2,1,0:T(8,128)} %copy-done.3) | copy-start | bytes 884740
  366.5 6.0 %copy-start.2 = (f32[4,24,768]{2,1,0:T(8,128)S(1)}, f32[4,24,768]{2,1,0:T(8,128)}, u32[]{:S(2)}) copy-start(f32[4,24,768]{2,1,0:T(8,128)} %copy-done.1) | copy-start | bytes 884740
  (36 other events, 40.0 us)

commit v2 on v0

v2 whole, which is shorter than its diff:
```python
import functools

import jax
import jax.numpy as jnp
from jax import lax
from jax.experimental import pallas as pl
from jax.experimental.pallas import tpu as pltpu
from jax.sharding import PartitionSpec as P

D = 768
HEAD_DIM = 64
SEQ = 197
HALF = 112
PAD = 2 * HALF
CAPACITY = 168
SLOTS = 176
EXPERTS = 4
NORM_EPSILON = 1e-06
MESH = pl.DeviceIdType.MESH
F32 = jnp.float32
BF16 = jnp.bfloat16


def dot(a, b):
    return lax.dot_general(a, b, (((1,), (0,)), ((), ())), preferred_element_type=F32)


def dot_nt(a, b):
    return lax.dot_general(a, b, (((1,), (1,)), ((), ())), preferred_element_type=F32)


def dot_tn(a, b):
    return lax.dot_general(a, b, (((0,), (0,)), ((), ())), preferred_element_type=F32)


def grid_device(y, z, x):
    return (lax.rem(y + 8, 4) * 4 + lax.rem(z + 8, 4)) * 2 + x


def normalize(v):
    center = v - jnp.mean(v, axis=-1, keepdims=True)
    spread = jnp.mean(center * center, axis=-1, keepdims=True)
    scale = lax.rsqrt(spread + NORM_EPSILON)
    return center * scale, scale


def norm_back(v, gain_row, upstream):
    nhat, scale = normalize(v)
    scaled = upstream * gain_row
    mean = jnp.mean(scaled, axis=-1, keepdims=True)
    along = jnp.mean(scaled * nhat, axis=-1, keepdims=True)
    dv = (scaled - mean - nhat * along) * scale
    gain_term = jnp.sum(upstream * nhat, axis=0, keepdims=True)
    bias_term = jnp.sum(upstream, axis=0, keepdims=True)
    return dv, gain_term, bias_term


def gelu_pair(h):
    phi = 0.5 * (1.0 + lax.erf(h * 0.7071067811865476))
    density = jnp.exp(-0.5 * h * h) * 0.3989422804014327
    return (h * phi).astype(BF16), phi + h * density


def head_mask(h, width):
    lane = lax.broadcasted_iota(jnp.int32, (1, width), 1)
    return jnp.logical_and(lane >= h * HEAD_DIM, lane < (h + 1) * HEAD_DIM)


def only(h, v):
    return jnp.where(head_mask(h, v.shape[1]), v, jnp.zeros((), v.dtype))


class TensorLinks:
    def __init__(self, refs, sems):
        self.full, self.pair_out, self.pair_in, self.far_out, self.far_in = refs
        self.sems = sems
        self.dp = lax.axis_index("dp")
        t = lax.axis_index("tensor")
        self.core = lax.rem(t, 2)
        self.other = t + 1 - 2 * self.core
        self.far = lax.rem(t + 2, 4)
        self.pairs, self.fars, self.gathers = {}, {}, {}

    def copy(self, source, target, slot, device):
        send, recv = self.sems
        c = pltpu.make_async_remote_copy(
            src_ref=source,
            dst_ref=target,
            send_sem=send.at[slot],
            recv_sem=recv.at[slot],
            device_id=(self.dp, device),
            device_id_type=MESH,
        )
        c.start()
        return c

    def share(self, ch, value):
        self.full[ch, 0] = value[:HALF]
        self.full[ch, 1] = value[HALF:]
        self.pair_out[ch] = self.full[ch, 1 - self.core].astype(BF16)
        self.pairs[ch] = self.copy(self.pair_out.at[ch], self.pair_in.at[ch], ch, self.other)

    def swap(self, ch, parity):
        self.pairs.pop(ch).wait()
        mine = self.full[ch, self.core] + self.pair_in[ch].astype(F32)
        self.far_out[ch] = mine.astype(BF16)
        self.fars[ch] = self.copy(
            self.far_out.at[ch], self.far_in.at[parity, ch], 4 + 4 * parity + ch, self.far
        )

    def total(self, ch, parity):
        self.fars.pop(ch).wait()
        return self.far_out[ch].astype(F32) + self.far_in[parity, ch].astype(F32)

    def gather(self, key, slot, ref):
        half = ref.at[self.core]
        self.gathers[key] = self.copy(half, half, 12 + slot, self.other)

    def arrived(self, key):
        self.gathers.pop(key).wait()


def attention_forward(n, win, wout, j, i, qkv, att, probs):
    q, k, v = (dot(n, win[3 * j + c]).astype(BF16) for c in range(3))
    for c, part in enumerate((q, k, v)):
        qkv[j, c, i] = part
    key = lax.broadcasted_iota(jnp.int32, (1, PAD), 1)
    mixed = None
    for h in range(3):
        s = dot_nt(only(h, q), k) * 0.125
        s = jnp.where(key < SEQ, s, -1e30)
        e = jnp.exp(s - jnp.max(s, axis=-1, keepdims=True))
        p = e * (1.0 / jnp.sum(e, axis=-1, keepdims=True))
        probs[j, i, h] = p
        term = dot(p.astype(BF16), only(h, v))
        mixed = term if mixed is None else mixed + term
    mixed = mixed.astype(BF16)
    att[j, i] = mixed
    return dot(mixed, wout[j])


def attention_backward(du, win, wout, j, i, qkv, att, probs, stack):
    q, k, v = (qkv[j, c, i] for c in range(3))
    d_att = dot_nt(du, wout[j]).astype(BF16)
    dq = dk = dv = None
    for h in range(3):
        p = probs[j, i, h]
        dp = dot_nt(only(h, d_att), v)
        ds = (p * (dp - jnp.sum(p * dp, axis=-1, keepdims=True))).astype(BF16)
        terms = (dot(ds, only(h, k)), dot_tn(ds, only(h, q)), dot_tn(p.astype(BF16), only(h, d_att)))
        dq, dk, dv = terms if dq is None else (a + b for a, b in zip((dq, dk, dv), terms))
    parts = [(dq * 0.125).astype(BF16), (dk * 0.125).astype(BF16), dv.astype(BF16)]
    stack[i * PAD : (i + 1) * PAD] = jnp.concatenate(parts + [att[j, i]], axis=1)
    return sum(dot_nt(part, win[3 * j + c]) for c, part in enumerate(parts))


def weight_grad(g, m, left, right):
    for s in range(2):
        out = dot_tn(left[:, s * 384 : (s + 1) * 384], right).astype(BF16)
        g[m, 2 * s : 2 * s + 2] = out.reshape(2, 4, 48, D)


def head_grad(g, m, n, du, stack):
    lane = lax.broadcasted_iota(jnp.int32, (1, 256), 1)
    last = stack[:, 512:]
    zero = jnp.zeros((), BF16)
    for s in range(2):
        cut = slice(s * 384, (s + 1) * 384)
        a = dot_tn(n[:, cut], stack[:, :512]).astype(BF16)
        b = dot_tn(n[:, cut], jnp.where(lane < 64, last, zero))
        b = (b + dot_tn(du[:, cut], jnp.where(lane < 64, zero, last))).astype(BF16)
        g[m, 2 * s : 2 * s + 2, :, :, 0:512] = a.reshape(2, 4, 48, 512)
        g[m, 2 * s : 2 * s + 2, :, :, 512:] = b.reshape(2, 4, 48, 256)


def forward_kernel(
    tokens, cot, gain, bias, win, wout, m1, m2, pick, spread, gate, ein, eout,
    out_o, n0, n1, n2, du2, qkv, att, probs, act, dgelu, streams, g2, terms, ge_o,
    n3, last, buf, drow, weighted, dbuf, eact, dhid, w_in, w_out, ge,
    full, pair_out, pair_in, far_out, far_in, send, recv, local_sem, grad_sem,
):
    links = TensorLinks((full, pair_out, pair_in, far_out, far_in), (send, recv))
    core = links.core
    barrier = pltpu.get_barrier_semaphore()
    for device in (links.other, links.far):
        pl.semaphore_signal(barrier, inc=1, device_id=(links.dp, device), device_id_type=MESH)
    loads = []
    for e in range(EXPERTS):
        for c, (source, target) in enumerate(((ein, w_in), (eout, w_out))):
            load = pltpu.make_async_copy(source.at[e], target.at[e], local_sem.at[2 * e + c])
            load.start()
            loads.append(load)

    def norm_rows(s, v):
        return (normalize(v)[0] * gain[s : s + 1] + bias[s : s + 1]).astype(BF16)

    for i in range(2):
        for half in range(2):
            n0[i, half] = norm_rows(0, tokens[i, half].astype(F32))
        streams[0, i] = tokens[i, core].astype(F32)

    def rows(ref, i):
        return ref[i].reshape(PAD, D)

    def block(s, i):
        if s != 1:
            return attention_forward(rows((n0, None, n2)[s], i), win, wout, s // 2, i, qkv, att, probs)
        hidden = dot(rows(n1, i), m1[...])
        act[i], dgelu[i] = gelu_pair(hidden)
        return dot(act[i], m2[...])

    normed = (n0, n1, n2, n3)

    def finish(s, i):
        v = streams[s, i] + links.total(i, s % 2)
        if s < 2:
            streams[s + 1, i] = v
        else:
            last[i] = v
        normed[s + 1][i, core] = norm_rows(s + 1, v)
        links.gather((s, i), 2 * s + i, normed[s + 1].at[i])

    steps = [(s, i) for s in range(3) for i in range(2)]
    for at, (s, i) in enumerate(steps):
        if s > 0:
            links.arrived((s - 1, i))
        term = block(s, i)
        if at == 0:
            pl.semaphore_wait(barrier, 2)
        links.share(i, term)
        links.swap(i, s % 2)
        if at > 0:
            finish(*steps[at - 1])
    finish(*steps[-1])

    drow[...] = (dot(pick[...], cot[...].reshape(2 * PAD, D)) * gate[...]).astype(BF16)
    for load in loads:
        load.wait()
    for i in range(2):
        links.arrived((2, i))
    buf[...] = dot(pick[...], n3[...].reshape(2 * PAD, D)).astype(BF16)
    for e in range(EXPERTS):
        cut = pl.ds(e * SLOTS, SLOTS)
        a, slope = gelu_pair(dot(buf[cut], w_in[e]))
        eact[cut] = a
        weighted[cut] = (dot(a, w_out[e]) * gate[cut]).astype(BF16)
        d = (slope * dot_nt(drow[cut], w_out[e])).astype(BF16)
        dhid[cut] = d
        dbuf[cut] = dot_nt(d, w_in[e]).astype(BF16)
    for i in range(2):
        links.share(i, dot(spread[i], dbuf[...]))
    for i in range(2):
        links.swap(i, 1)
    for i in range(2):
        links.share(2 + i, dot(spread[i], weighted[...]))
    for i in range(2):
        links.swap(2 + i, 1)
    copies = []

    def expert_grads(e):
        cut = pl.ds(e * SLOTS, SLOTS)
        for m, left, right in ((e, buf, dhid), (EXPERTS + e, drow, eact)):
            weight_grad(ge, m, left[cut], right[cut])
            copy = pltpu.make_async_copy(ge.at[m], ge_o.at[m], grad_sem.at[m])
            copy.start()
            copies.append(copy)

    expert_grads(0)
    expert_grads(1)
    gains = biases = 0.0
    for i in range(2):
        dv, gain_term, bias_term = norm_back(last[i], gain[3:4], links.total(i, 1))
        gains, biases = gains + gain_term, biases + bias_term
        g = cot[i, core].astype(F32) + dv
        g2[i] = g
        du2[i, core] = g.astype(BF16)
        links.gather((3, i), 6 + i, du2.at[i])
    terms[...] = jnp.zeros_like(terms)
    terms[3:4] = gains
    terms[7:8] = biases
    for i in range(2):
        out_o[i, core] = last[i] + links.total(2 + i, 1)
        links.gather((4, i), 8 + i, out_o.at[i])
    expert_grads(2)
    expert_grads(3)
    for i in range(2):
        links.arrived((3, i))
        links.arrived((4, i))
    for copy in copies:
        copy.wait()


class ImageSum:
    def __init__(self, spec, refs, sems, base, place, out):
        self.mats, self.width, self.order, self.ring, self.held = spec
        self.refs, self.sems, self.base, self.place, self.out = refs, sems, base, place, out
        self.copies = {}

    def send(self, name, slot, source, target, axis, k):
        y, z, x, t = self.place
        if axis == "x":
            device = grid_device(y, z, 1 - x)
        else:
            device = grid_device(y + k, z, x) if axis == "y" else grid_device(y, z + k, x)
        send, recv = self.sems
        c = pltpu.make_async_remote_copy(
            src_ref=source,
            dst_ref=target,
            send_sem=send.at[self.base + slot],
            recv_sem=recv.at[self.base + slot],
            device_id=(device, t),
            device_id_type=MESH,
        )
        c.start()
        self.copies.setdefault(name, []).append(c)

    def wait(self, name):
        for c in self.copies.pop(name, []):
            c.wait()

    def block(self, k):
        source, y, z = self.source, self.place[0], self.place[1]
        if self.order == "y":
            return source.at[:, lax.rem(y + k, 4)]
        return source.at[:, :, lax.rem(z + k, 4)]

    def start(self, source):
        self.source = source
        axis, h = self.order, self.width // 2
        r = self.refs
        low, high = pl.ds(0, h), pl.ds(h, h)
        if self.ring:
            far = self.block(2)
            self.send("a", 0, far.at[:, :, :, low], r["ra"].at[0], axis, 1)
            self.send("a", 1, far.at[:, :, :, high], r["ra"].at[1], axis, 3)
            self.send("b", 2, self.block(1).at[:, :, :, high], r["rb"].at[0, :, :, :, high], axis, 1)
            self.send("b", 3, self.block(3).at[:, :, :, low], r["rb"].at[1, :, :, :, low], axis, 3)
        else:
            for k in (2, 1, 3):
                self.send("b", k, self.block(k), r["rb"].at[k - 1], axis, k)
        if not self.held:
            y, z, x, t = self.place
            pieces = [
                (self.block(0), r["own"]),
                (self.block(1).at[:, :, :, low], r["near"].at[0]),
                (self.block(3).at[:, :, :, high], r["near"].at[1]),
            ]
            for i, (a, b) in enumerate(pieces):
                c = pltpu.make_async_copy(a, b, r["local"].at[i])
                c.start()
                self.copies.setdefault("own", []).append(c)

    def middle(self):
        r, h = self.refs, self.width // 2
        low, high = pl.ds(0, h), pl.ds(h, h)
        self.wait("a")
        self.wait("own")
        for side, k, cut in ((0, 1, low), (1, 3, high)):
            near = r["near"].at[side] if not self.held else self.block(k).at[:, :, :, cut]

            def add(m, carry, near=near, side=side):
                for b in range(4):
                    r["ra"][side, m, b] = (r["ra"][side, m, b].astype(F32) + near[m, b].astype(F32)).astype(BF16)
                return carry

            lax.fori_loop(0, self.mats, add, 0)
        self.send("b", 4, r["ra"].at[0], r["rb"].at[0, :, :, :, low], self.order, 1)
        self.send("b", 5, r["ra"].at[1], r["rb"].at[1, :, :, :, high], self.order, 3)

    def second(self):
        r = self.refs
        self.wait("b")
        own = self.block(0) if self.held else r["own"]

        def add(m, carry):
            for b in range(4):
                acc = own[m, b].astype(F32)
                for k in range(2 if self.ring else 3):
                    acc = acc + r["rb"][k, m, b].astype(F32)
                r["s1"][m, b] = acc.astype(BF16)
            return carry

        lax.fori_loop(0, self.mats, add, 0)
        axis = "z" if self.order == "y" else "y"
        mine = self.place[1] if axis == "z" else self.place[0]
        for k in (2, 1, 3):
            self.send("c", 5 + k, r["s1"].at[:, lax.rem(mine + k, 4)], r["rc"].at[k - 1], axis, k)

    def third(self):
        r = self.refs
        y, z, x, t = self.place
        mine = z if self.order == "y" else y
        self.wait("c")
        other = pl.ds(pl.multiple_of((1 - x) * 24, 8), 24)
        for m in range(self.mats):
            acc = r["s1"][m, mine].astype(F32)
            for k in range(3):
                acc = acc + r["rc"][k, m].astype(F32)
            r["tot"][m] = acc
        for m in range(0, self.mats, 2):
            pieces = [r["tot"][n, other] for n in (m, min(m + 1, self.mats - 1))]
            r["xs"][m // 2] = jnp.concatenate(pieces, axis=0).astype(BF16)
        self.send("d", 9, r["xs"], r["xr"], "x", 0)

    def finish(self):
        r = self.refs
        x = self.place[2]
        self.wait("d")
        mine = pl.ds(pl.multiple_of(x * 24, 8), 24)
        for m in range(self.mats):
            theirs = r["xr"][m // 2].astype(F32)
            self.out(m, r["tot"][m, mine] + theirs[24 * (m % 2) : 24 * (m % 2) + 24])


GROUPS = {
    "e0": (4, 768, "y", True, False),
    "e1": (4, 768, "z", True, False),
    "m0": (1, 768, "y", True, True),
    "m1": (1, 768, "z", True, True),
    "a1y": (1, 384, "y", False, True),
    "a1z": (1, 384, "z", False, True),
    "a0y": (1, 384, "y", False, True),
    "a0z": (1, 384, "z", False, True),
    "n": (1, 128, "y", False, True),
}


def group_scratch(spec):
    mats, width, order, ring, held = spec
    pairs = (mats + 1) // 2
    shapes = {
        "rb": pltpu.VMEM((2 if ring else 3, mats, 4, 48, width), BF16),
        "s1": pltpu.VMEM((mats, 4, 48, width), BF16),
        "rc": pltpu.VMEM((3, mats, 48, width), BF16),
        "tot": pltpu.VMEM((mats, 48, width), F32),
        "xs": pltpu.VMEM((pairs, 48, width), BF16),
        "xr": pltpu.VMEM((pairs, 48, width), BF16),
    }
    if ring:
        shapes["ra"] = pltpu.VMEM((2, mats, 4, 48, width // 2), BF16)
    if not held:
        shapes["own"] = pltpu.VMEM((mats, 4, 48, width), BF16)
        shapes["near"] = pltpu.VMEM((2, mats, 4, 48, width // 2), BF16)
        shapes["local"] = pltpu.SemaphoreType.DMA((3,))
    return shapes


BACK_IN = 18


def backward_kernel(*refs):
    (
        n0, n1, n2, du2, qkv, att, probs, act, dgelu, streams, g2, terms,
        gain, win, wout, m1, m2, ge,
    ) = refs[:BACK_IN]
    token_o, e_o, d_o, norm_o = refs[BACK_IN : BACK_IN + 4]
    rest = list(refs[BACK_IN + 4 :])
    (
        du1, du0, stack, dhid, g, gn, sums, sums_in, full, pair_out, pair_in, far_out, far_in,
        send, recv, group_send, group_recv,
    ) = rest[:17]
    rest = rest[17:]
    links = TensorLinks((full, pair_out, pair_in, far_out, far_in), (send, recv))
    core = links.core
    dp = links.dp
    t = lax.axis_index("tensor")
    y, z, x = dp // 8, lax.rem(dp // 2, 4), lax.rem(dp, 2)
    place = (y, z, x, t)

    def out_at(ref, base, cut):
        def store(m, value):
            ref[base + m, :, cut] = value

        return store

    everything = slice(None)
    outs = {
        "e0": out_at(e_o, 0, everything),
        "e1": out_at(e_o, 4, everything),
        "m0": out_at(d_o, 0, everything),
        "m1": out_at(d_o, 1, everything),
        "a1y": out_at(d_o, 3, slice(0, 384)),
        "a1z": out_at(d_o, 3, slice(384, 768)),
        "a0y": out_at(d_o, 2, slice(0, 384)),
        "a0z": out_at(d_o, 2, slice(384, 768)),
        "n": out_at(norm_o, 0, everything),
    }
    groups = {}
    for at, (name, spec) in enumerate(GROUPS.items()):
        keys = list(group_scratch(spec))
        held = dict(zip(keys, rest[: len(keys)]))
        rest = rest[len(keys) :]
        groups[name] = ImageSum(spec, held, (group_send, group_recv), 10 * at, place, outs[name])

    barrier = pltpu.get_barrier_semaphore()
    for device in ((dp, links.other), (dp, links.far), (grid_device(y, z, 1 - x), t)):
        pl.semaphore_signal(barrier, inc=1, device_id=device, device_id_type=MESH)
    for k in (1, 2, 3):
        for device in (grid_device(y + k, z, x), grid_device(y, z + k, x)):
            pl.semaphore_signal(barrier, inc=1, device_id=(device, t), device_id_type=MESH)
    pl.semaphore_wait(barrier, 9)

    groups["e0"].start(ge.at[0:4])
    groups["e1"].start(ge.at[4:8])
    sums[...] = terms[...]

    def rows(ref, i):
        return ref[i].reshape(PAD, D)

    def flat(ref):
        return ref[...].reshape(2 * PAD, D)

    def share(parity, i, value):
        links.share(i, value)
        links.swap(i, parity)

    def finish(s, parity, i, target, slot):
        dv, gain_term, bias_term = norm_back(streams[s, i], gain[s : s + 1], links.total(i, parity))
        sums[s : s + 1] = sums[s : s + 1] + gain_term
        sums[4 + s : 5 + s] = sums[4 + s : 5 + s] + bias_term
        v = g2[i] + dv
        if s > 0:
            g2[i] = v
            target[i, core] = v.astype(BF16)
        else:
            target[i, core] = v
        links.gather((s, i), 2 * s + slot, target.at[i])

    for i in range(2):
        share(0, i, attention_backward(rows(du2, i), win, wout, 1, i, qkv, att, probs, stack))
    head_grad(g, 3, flat(n2), flat(du2), stack)
    groups["a1y"].start(g.at[3:4, :, :, :, 0:384])
    groups["a1z"].start(g.at[3:4, :, :, :, 384:768])
    for i in range(2):
        finish(2, 0, i, du1, i)

    for i in range(2):
        links.arrived((2, i))
        d = (dgelu[i] * dot_nt(rows(du1, i), m2[...])).astype(BF16)
        dhid[i] = d
        share(1, i, dot_nt(d, m1[...]))
    weight_grad(g, 0, flat(n1), dhid[...].reshape(2 * PAD, D))
    groups["m0"].start(g.at[0:1])
    weight_grad(g, 1, flat(du1), act[...].reshape(2 * PAD, D))
    groups["m1"].start(g.at[1:2])
    for i in range(2):
        finish(1, 1, i, du0, i)

    for i in range(2):
        links.arrived((1, i))
        share(0, i, attention_backward(rows(du0, i), win, wout, 0, i, qkv, att, probs, stack))
    groups["e0"].middle()
    groups["e1"].middle()
    head_grad(g, 2, flat(n0), flat(du0), stack)
    groups["a0y"].start(g.at[2:3, :, :, :, 0:384])
    groups["a0z"].start(g.at[2:3, :, :, :, 384:768])
    for i in range(2):
        finish(0, 0, i, token_o, i)
    both = links.copy(sums, sums_in, 18, links.other)
    groups["a1y"].second()
    groups["a1z"].second()
    groups["m0"].middle()
    groups["m1"].middle()
    both.wait()
    wide = jnp.concatenate([sums[...] + sums_in[...], jnp.zeros((120, D), F32)], axis=0)
    gn[0] = wide.T.astype(BF16).reshape(4, 4, 48, 128)
    groups["n"].start(gn)
    for name in ("e0", "e1", "a0y", "a0z", "m0", "m1", "n"):
        groups[name].second()
    for name in ("a1y", "a1z", "e0", "e1", "a0y", "a0z", "m0", "m1", "n"):
        groups[name].third()
    for name in ("a1y", "a1z", "e0", "e1", "a0y", "a0z", "m0", "m1", "n"):
        groups[name].finish()
    for i in range(2):
        links.arrived((0, i))


def link_scratch(channels, sems):
    return [
        pltpu.VMEM((channels, 2, HALF, D), F32),
        pltpu.VMEM((channels, HALF, D), BF16),
        pltpu.VMEM((channels, HALF, D), BF16),
        pltpu.VMEM((channels, HALF, D), BF16),
        pltpu.VMEM((2, channels, HALF, D), BF16),
        pltpu.SemaphoreType.DMA((sems,)),
        pltpu.SemaphoreType.DMA((sems,)),
    ]


def padded(v):
    v = v.reshape(2, SEQ, -1)
    v = jnp.pad(v, ((0, 0), (0, PAD - SEQ), (0, 0)))
    return v.reshape(2, 2, HALF, v.shape[-1])


def unpadded(v):
    return v.reshape(2, PAD, D)[:, :SEQ].reshape(2 * SEQ, D)


def local(
    tokens,
    norm_gain,
    norm_bias,
    attn_in,
    attn_out,
    mlp_in,
    mlp_out,
    expert_in,
    expert_out,
    routes,
    slot_index,
    gate_weights,
    cotangent,
):
    head_width = attn_out.shape[1]
    kept = slot_index < CAPACITY
    index = jnp.where(kept, routes * SLOTS + slot_index, -1)
    index = jnp.pad(index.reshape(2, SEQ, 2), ((0, 0), (0, PAD - SEQ), (0, 0)), constant_values=-1)
    gates = jnp.pad(gate_weights.reshape(2, SEQ, 2), ((0, 0), (0, PAD - SEQ), (0, 0)))
    slots = EXPERTS * SLOTS
    flat = index.reshape(2 * PAD, 2)
    number = lax.broadcasted_iota(jnp.int32, (slots, 2 * PAD), 0)
    hits = [number == flat[:, k][None, :] for k in range(2)]
    pick = jnp.logical_or(*hits).astype(BF16)
    gate = sum(
        jnp.sum(jnp.where(hits[k], gates.reshape(2 * PAD, 2)[:, k][None, :], 0.0), axis=1, keepdims=True)
        for k in range(2)
    )
    number = lax.broadcasted_iota(jnp.int32, (2, PAD, slots), 2)
    spread = jnp.logical_or(number == index[:, :, :1], number == index[:, :, 1:]).astype(BF16)

    whole = pl.BlockSpec(memory_space=pltpu.VMEM)
    hbm = pl.BlockSpec(memory_space=pl.ANY)
    shape = jax.ShapeDtypeStruct
    half_rows = (2, 2, HALF, D)
    win = attn_in.reshape(6, D, head_width)
    (out, n0, n1, n2, du2, qkv, att, probs, act, dgelu, streams, g2, terms, ge) = pl.pallas_call(
        forward_kernel,
        out_shape=[
            shape(half_rows, F32),
            shape(half_rows, BF16),
            shape(half_rows, BF16),
            shape(half_rows, BF16),
            shape(half_rows, BF16),
            shape((2, 3, 2, PAD, head_width), BF16),
            shape((2, 2, PAD, head_width), BF16),
            shape((2, 2, 3, PAD, PAD), F32),
            shape((2, PAD, D), BF16),
            shape((2, PAD, D), F32),
            shape((3, 2, HALF, D), F32),
            shape((2, HALF, D), F32),
            shape((8, D), F32),
            shape((2 * EXPERTS, 4, 4, 48, D), BF16),
        ],
        in_specs=[whole] * 11 + [hbm] * 2,
        out_specs=[whole] * 13 + [hbm],
        scratch_shapes=[
            pltpu.VMEM(half_rows, BF16),
            pltpu.VMEM((2, HALF, D), F32),
        ]
        + [pltpu.VMEM((slots, D), BF16)] * 6
        + [
            pltpu.VMEM((EXPERTS, D, D), BF16),
            pltpu.VMEM((EXPERTS, D, D), BF16),
            pltpu.VMEM((2 * EXPERTS, 4, 4, 48, D), BF16),
        ]
        + link_scratch(4, 22)
        + [pltpu.SemaphoreType.DMA((8,)), pltpu.SemaphoreType.DMA((8,))],
        compiler_params=pltpu.CompilerParams(
            collective_id=1, has_side_effects=True, vmem_limit_bytes=60 << 20
        ),
        name="forward",
    )(
        padded(tokens), padded(cotangent), norm_gain, norm_bias, win, attn_out, mlp_in, mlp_out,
        pick, spread, gate, expert_in, expert_out,
    )

    scratch = (
        [
            pltpu.VMEM(half_rows, BF16),
            pltpu.VMEM(half_rows, BF16),
            pltpu.VMEM((2 * PAD, D), BF16),
            pltpu.VMEM((2, PAD, D), BF16),
            pltpu.VMEM((4, 4, 4, 48, D), BF16),
            pltpu.VMEM((1, 4, 4, 48, 128), BF16),
            pltpu.VMEM((8, D), F32),
            pltpu.VMEM((8, D), F32),
        ]
        + link_scratch(2, 20)
        + [
            pltpu.SemaphoreType.DMA((10 * len(GROUPS),)),
            pltpu.SemaphoreType.DMA((10 * len(GROUPS),)),
        ]
    )
    for spec in GROUPS.values():
        scratch += list(group_scratch(spec).values())
    token_grad, experts, dense, norms = pl.pallas_call(
        backward_kernel,
        out_shape=[
            shape(half_rows, F32),
            shape((2 * EXPERTS, 24, D), F32),
            shape((4, 24, D), F32),
            shape((1, 24, 128), F32),
        ],
        in_specs=[whole] * (BACK_IN - 1) + [hbm],
        out_specs=[whole] * 4,
        scratch_shapes=scratch,
        compiler_params=pltpu.CompilerParams(
            collective_id=2, has_side_effects=True, vmem_limit_bytes=60 << 20
        ),
        name="backward",
    )(
        n0, n1, n2, du2, qkv, att, probs, act, dgelu, streams, g2, terms,
        norm_gain, win, attn_out, mlp_in, mlp_out, ge,
    )
    heads = dense[2:]
    attn_in_sum = jnp.stack(
        [heads[:, :, c * head_width : (c + 1) * head_width] for c in range(3)], axis=1
    )
    return (
        unpadded(out),
        unpadded(token_grad),
        norms[0, :, :4].T,
        norms[0, :, 4:8].T,
        attn_in_sum,
        jnp.swapaxes(heads[:, :, 3 * head_width :], 1, 2),
        dense[0],
        dense[1].T,
        experts[:EXPERTS],
        jnp.swapaxes(experts[EXPERTS:], 1, 2),
    )


def solution(mesh):
    placed = (
        P("dp", None),
        P(),
        P(),
        P(None, None, None, "tensor"),
        P(None, "tensor", None),
        P(None, "tensor"),
        P("tensor", None),
        P(None, None, "tensor"),
        P(None, "tensor", None),
        P("dp", None),
        P("dp", None),
        P("dp", None),
        P("dp", None),
    )
    return jax.shard_map(
        local,
        mesh=mesh,
        in_specs=placed,
        out_specs=(
            P("dp", None),
            P("dp", None),
            P(None, "dp"),
            P(None, "dp"),
            P(None, None, "dp", "tensor"),
            P(None, "tensor", "dp"),
            P("dp", "tensor"),
            P("tensor", "dp"),
            P(None, "dp", "tensor"),
            P(None, "tensor", "dp"),
        ),
        check_vma=False,
    )
```

time: 1490 us -> 197 us (0.13)
  waiting for transfers between devices: 1030 us -> 0 us
  Pallas kernels: 0 us -> 177 us
  blocking collectives: 158 us -> 0 us
  local copies, waits for them, and re-layouts: 163 us -> 14.9 us
  matrix products: 59.7 us -> 0 us
  other arithmetic: 51.8 us -> 3.45 us
  between operations: 17 us -> 0.77 us
    unnamed x15 -> x0, waiting for transfers between devices: 674 us -> none
    psum x7 -> x0, waiting for transfers between devices: 201 us -> none  [the longest x2 49.2 us: head_forward(): mixed_total = lax.psum(partial_sum, 'tensor')]
    pallas_call x0 -> x2, Pallas kernels: none -> 177 us  [the longest x1 104 us: local(): pl.pallas_call(backward_kernel, out_shape=[shape(half_rows, F32), shape((...]
    unnamed x1 -> x0, blocking collectives: 158 us -> none
    reduce_scatter x2 -> x0, waiting for transfers between devices: 156 us -> none  [the longest x1 156 us: local(): lax.psum_scatter(grad_mlp_in.astype(jnp.bfloat16), 'dp', scatter_dimensio...]
    scatter x2 -> x0, local copies, waits for them, and re-layouts: 80.8 us -> none  [the longest x1 40.4 us: expert_tables(): owner_table = jnp.full((expert_count, CAPACITY + 1), row_count, jnp.int32...]
    dot_general x34 -> x0, matrix products: 58.1 us -> none  [the longest x2 5.56 us: head_backward(): jnp.einsum('jne,jde->nd', d_projected, weight_in, preferred_element_type=...]
    reduce_sum x24 -> x1, other arithmetic: 31.6 us -> 0.42 us  [local(): jnp.sum(jnp.where(hits[k], gates.reshape(2 * PAD, 2)[:, k][None, :], 0.0)...]
  transfers between devices with their start and end apart: 12 -> 0, of which waited for: 9 -> 0; matrix products, arithmetic and copies ran while one was open for 11% -> 0% of each run, Pallas kernels for 0% -> 0%
where the time goes in v2:
time: 197 us; the launch traced here: 196 us
  Pallas kernels  177 us (90%)
  local copies, waits for them, and re-layouts  14.9 us (8%)
  other arithmetic  3.45 us (2%)
    pallas_call x1, Pallas kernels, local(): pl.pallas_call(backward_kernel, out_shape=[shape(half_rows, F32), shape((...  104 us
    pallas_call x1, Pallas kernels, local(): pl.pallas_call(forward_kernel, out_shape=[shape(half_rows, F32), shape(ha...  73.6 us

profile of v2, /device:TPU:0, one launch (start us, length us, event | category | flops | bytes accessed | tf_op | source)
XLA Modules:
  0.0 196.4 jit_solution(14647470773620982229)
XLA Ops:
  0.6 0.7 compare_select_fusion
  1.4 0.1 reshape.82
  1.4 0.1 reshape.83
  1.6 0.8 reshape.84
  2.3 0.1 reshape.85
  2.4 0.4 select_reduce_fusion
  2.9 0.0 copy-start.3
  2.9 0.9 add.19.gate
  3.8 1.2 reshape.77
  5.0 0.9 pad.15
  5.9 0.0 copy-done.3
  5.9 0.1 reshape.79
  6.0 0.0 copy-start
  6.0 0.9 pad.16
  6.9 1.1 fusion.3.spread
  8.0 1.2 fusion.1.pick
  9.2 0.0 copy-done
  9.2 2.5 %copy.27 = bf16[2,3,768,192]{3,2,1,0:T(8,128)(2,1)} copy(bf16[2,3,768,192]{2,3,1,0:T(8,128)(2,1)S(1)} %copy-done) | data formatting | bytes 3538944 | tf_op args[3]
  11.7 73.6 %forward.1 = (f32[2,2,112,768]{3,2,1,0:T(8,128)}, bf16[2,2,112,768]{3,2,1,0:T(8,128)(2,1)}, bf16[2,2,112,768]{3,2,1,0:T(8,128)(2,1)}, bf16[2,2,112,768]{3,2,1,0:...) custom-call(bf16[2,2,112,768]{3,2,1,0:T(8,128)(2,1)} %bitcast.45, ...), custom_call_target="tpu_custom_call" | custom-call | tf_op jit(solution)/shard_map/forward/pallas_call | solution.py:637
  85.3 0.0 copy-start.1
  85.3 103.6 %backward.1 = (f32[2,2,112,768]{3,2,1,0:T(8,128)}, f32[8,24,768]{2,1,0:T(8,128)}, f32[4,24,768]{2,1,0:T(8,128)}, f32[1,24,128]{2,1,0:T(8,128)}) custom-call(bf16[2,2,112,768]{3,2,1,0:T(8,128)(2,1)} %get-tuple-element.29.refs_0_, bf16[2,2,112,768]{3,2,1,0:T(8,128)(2,1)} %get-tuple-element.30.refs_1_, bf16[2,2,112,768]{3,2,1,0:T(8,128)(2,1)} %get-tuple-element.31.refs_2_, ...), custom_call_target="tpu_custom_call" | custom-call | tf_op jit(solution)/shard_map/backward/pallas_call | solution.py:697
  189.0 0.0 copy-done.1
  189.0 0.1 slice.81
  189.1 0.0 copy-start.2
  189.1 1.1 reshape.87
  190.2 0.6 copy-done.2
  190.8 0.1 slice.82
  190.9 0.0 copy-start.6
  190.9 0.0 copy-start.5
  190.9 0.0 copy-start.4
  191.0 1.1 reshape.89
  192.1 0.0 copy-done.6
  192.1 0.1 fusion.4
  192.2 0.7 copy.30
  192.8 0.7 copy.29
  193.5 0.0 copy-done.5
  193.5 0.7 slice_bitcast_fusion.1
  194.2 0.7 slice_bitcast_fusion.3
  194.9 0.7 copy.31
  195.5 0.0 copy-done.4
  195.5 0.8 slice_bitcast_fusion
  (7 shorter events, 0.1 us)
Async XLA Ops:
  2.9 3.0 %copy-start.3 = (bf16[394,768]{1,0:T(8,128)(2,1)S(1)}, bf16[394,768]{1,0:T(8,128)(2,1)}, u32[]{:S(2)}) copy-start(bf16[394,768]{1,0:T(8,128)(2,1)} %param.25) | copy-start | bytes 1815556
  6.0 3.2 %copy-start = (bf16[2,3,768,192]{2,3,1,0:T(8,128)(2,1)S(1)}, bf16[2,3,768,192]{2,3,1,0:T(8,128)(2,1)}, u32[]{:S(2)}) copy-start(bf16[2,3,768,192]{2,3,1,0:T(8,128)(2,1)} %param.16) | copy-start | bytes 5308420
  85.3 103.6 %copy-start.1 = (f32[2,2,112,768]{3,2,1,0:T(8,128)S(1)}, f32[2,2,112,768]{3,2,1,0:T(8,128)}, u32[]{:S(2)}) copy-start(f32[2,2,112,768]{3,2,1,0:T(8,128)} %get-tuple-element.28) | copy-start | bytes 4128772
  189.1 1.8 copy-start.2
  190.9 1.2 copy-start.6
  190.9 2.6 %copy-start.5 = (f32[4,24,768]{2,1,0:T(8,128)S(1)}, f32[4,24,768]{2,1,0:T(8,128)}, u32[]{:S(2)}) copy-start(f32[4,24,768]{2,1,0:T(8,128)} %get-tuple-element.44) | copy-start | bytes 884740
  190.9 4.6 %copy-start.4 = (f32[8,24,768]{2,1,0:T(8,128)S(1)}, f32[8,24,768]{2,1,0:T(8,128)}, u32[]{:S(2)}) copy-start(f32[8,24,768]{2,1,0:T(8,128)} %get-tuple-element.45) | copy-start | bytes 1769476

commit v3 on v2

--- a/solution.py
+++ b/solution.py
@@ -79,7 +79,7 @@
         self.core = lax.rem(t, 2)
         self.other = t + 1 - 2 * self.core
         self.far = lax.rem(t + 2, 4)
-        self.pairs, self.fars, self.gathers = {}, {}, {}
+        self.pairs, self.fars, self.gathers, self.mine = {}, {}, {}, {}
 
     def copy(self, source, target, slot, device):
         send, recv = self.sems
@@ -99,29 +99,55 @@
         self.full[ch, 1] = value[HALF:]
         self.pair_out[ch] = self.full[ch, 1 - self.core].astype(BF16)
         self.pairs[ch] = self.copy(self.pair_out.at[ch], self.pair_in.at[ch], ch, self.other)
+        self.mine[ch] = lambda: self.full[ch, self.core]
+
+    def share_held(self, ch, ref):
+        self.pairs[ch] = self.copy(ref.at[1 - self.core], self.pair_in.at[ch], ch, self.other)
+        self.mine[ch] = lambda: ref[self.core].astype(F32)
+
+    def place(self, ch, parity):
+        return 2 * parity + ch if ch < 2 else 2 + ch
 
     def swap(self, ch, parity):
         self.pairs.pop(ch).wait()
-        mine = self.full[ch, self.core] + self.pair_in[ch].astype(F32)
+        mine = self.mine.pop(ch)() + self.pair_in[ch].astype(F32)
         self.far_out[ch] = mine.astype(BF16)
-        self.fars[ch] = self.copy(
-            self.far_out.at[ch], self.far_in.at[parity, ch], 4 + 4 * parity + ch, self.far
-        )
+        at = self.place(ch, parity)
+        self.fars[ch] = self.copy(self.far_out.at[ch], self.far_in.at[at], 4 + at, self.far)
 
     def total(self, ch, parity):
         self.fars.pop(ch).wait()
-        return self.far_out[ch].astype(F32) + self.far_in[parity, ch].astype(F32)
+        return self.far_out[ch].astype(F32) + self.far_in[self.place(ch, parity)].astype(F32)
 
     def gather(self, key, slot, ref):
         half = ref.at[self.core]
-        self.gathers[key] = self.copy(half, half, 12 + slot, self.other)
+        self.gathers[key] = self.copy(half, half, 10 + slot, self.other)
 
     def arrived(self, key):
         self.gathers.pop(key).wait()
 
 
+class Loads:
+    def __init__(self, sems):
+        self.sems, self.pending, self.count = sems, {}, 0
+
+    def start(self, key, source, target):
+        c = pltpu.make_async_copy(source, target, self.sems.at[self.count])
+        c.start()
+        self.count += 1
+        self.pending[key] = c
+
+    def need(self, *keys):
+        for key in keys:
+            if key in self.pending:
+                self.pending.pop(key).wait()
+
+    def drain(self):
+        self.need(*list(self.pending))
+
+
 def attention_forward(n, win, wout, j, i, qkv, att, probs):
-    q, k, v = (dot(n, win[3 * j + c]).astype(BF16) for c in range(3))
+    q, k, v = (dot_nt(n, win[3 * j + c]).astype(BF16) for c in range(3))
     for c, part in enumerate((q, k, v)):
         qkv[j, c, i] = part
     key = lax.broadcasted_iota(jnp.int32, (1, PAD), 1)
@@ -151,7 +177,7 @@
         dq, dk, dv = terms if dq is None else (a + b for a, b in zip((dq, dk, dv), terms))
     parts = [(dq * 0.125).astype(BF16), (dk * 0.125).astype(BF16), dv.astype(BF16)]
     stack[i * PAD : (i + 1) * PAD] = jnp.concatenate(parts + [att[j, i]], axis=1)
-    return sum(dot_nt(part, win[3 * j + c]) for c, part in enumerate(parts))
+    return sum(dot(part, win[3 * j + c]) for c, part in enumerate(parts))
 
 
 def weight_grad(g, m, left, right):
@@ -173,31 +199,72 @@
         g[m, 2 * s : 2 * s + 2, :, :, 512:] = b.reshape(2, 4, 48, 256)
 
 
+KEPT = ("n0", "n1", "n2", "cotp", "qkv", "att", "probs", "act", "dgelu", "streams", "dn", "mo")
+
+
+def kept_shapes(head_width):
+    half_rows = (2, 2, HALF, D)
+    return {
+        "n0": (half_rows, BF16),
+        "n1": (half_rows, BF16),
+        "n2": (half_rows, BF16),
+        "cotp": (half_rows, BF16),
+        "qkv": ((2, 3, 2, PAD, head_width), BF16),
+        "att": ((2, 2, PAD, head_width), BF16),
+        "probs": ((2, 2, 3, PAD, PAD), F32),
+        "act": ((2, PAD, D), BF16),
+        "dgelu": ((2, PAD, D), F32),
+        "streams": ((4, 2, HALF, D), F32),
+        "dn": (half_rows, BF16),
+        "mo": (half_rows, BF16),
+    }
+
+
 def forward_kernel(
-    tokens, cot, gain, bias, win, wout, m1, m2, pick, spread, gate, ein, eout,
-    out_o, n0, n1, n2, du2, qkv, att, probs, act, dgelu, streams, g2, terms, ge_o,
-    n3, last, buf, drow, weighted, dbuf, eact, dhid, w_in, w_out, ge,
-    full, pair_out, pair_in, far_out, far_in, send, recv, local_sem, grad_sem,
+    tokens, cot, routes, slots, gates, gain, bias, win, wout, m1_h, m2_h, ein, eout, *refs
 ):
+    outs = dict(zip(KEPT, refs))
+    ge_o = refs[len(KEPT)]
+    refs = refs[len(KEPT) + 1 :]
+    kept = dict(zip(KEPT, refs))
+    (
+        n3, pick, spread, gate, buf, drow, weighted, dbuf, eact, dhid, m1, m2, w_in, w_out, ge,
+        full, pair_out, pair_in, far_out, far_in, send, recv, load_sem, save_sem,
+    ) = refs[len(KEPT) :]
+    n0, n1, n2, cotp, qkv, att, probs, act, dgelu, streams, dn, mo = (kept[k] for k in KEPT)
     links = TensorLinks((full, pair_out, pair_in, far_out, far_in), (send, recv))
     core = links.core
     barrier = pltpu.get_barrier_semaphore()
     for device in (links.other, links.far):
         pl.semaphore_signal(barrier, inc=1, device_id=(links.dp, device), device_id_type=MESH)
-    loads = []
+    loads, saves = Loads(load_sem), Loads(save_sem)
+    loads.start("m1", m1_h, m1)
+    loads.start("m2", m2_h, m2)
     for e in range(EXPERTS):
-        for c, (source, target) in enumerate(((ein, w_in), (eout, w_out))):
-            load = pltpu.make_async_copy(source.at[e], target.at[e], local_sem.at[2 * e + c])
-            load.start()
-            loads.append(load)
+        loads.start(("in", e), ein.at[e], w_in.at[e])
+        loads.start(("out", e), eout.at[e], w_out.at[e])
+
+    rows_of = tokens.shape[0]
+
+    def placement():
+        row = lax.broadcasted_iota(jnp.int32, (2 * PAD, rows_of), 0)
+        column = lax.broadcasted_iota(jnp.int32, (2 * PAD, rows_of), 1)
+        image = (row >= PAD).astype(jnp.int32)
+        inside = row - image * PAD < SEQ
+        hit = jnp.logical_and(inside, column == row - image * (PAD - SEQ))
+        return jnp.where(hit, 1.0, 0.0).astype(BF16)
+
+    def padded(ref):
+        return dot(placement(), ref[...]).astype(BF16).reshape(2, 2, HALF, D)
 
     def norm_rows(s, v):
         return (normalize(v)[0] * gain[s : s + 1] + bias[s : s + 1]).astype(BF16)
 
+    mo[...] = padded(tokens)
     for i in range(2):
         for half in range(2):
-            n0[i, half] = norm_rows(0, tokens[i, half].astype(F32))
-        streams[0, i] = tokens[i, core].astype(F32)
+            n0[i, half] = norm_rows(0, mo[i, half].astype(F32))
+        streams[0, i] = mo[i, core].astype(F32)
 
     def rows(ref, i):
         return ref[i].reshape(PAD, D)
@@ -205,6 +272,7 @@
     def block(s, i):
         if s != 1:
             return attention_forward(rows((n0, None, n2)[s], i), win, wout, s // 2, i, qkv, att, probs)
+        loads.need("m1", "m2")
         hidden = dot(rows(n1, i), m1[...])
         act[i], dgelu[i] = gelu_pair(hidden)
         return dot(act[i], m2[...])
@@ -213,13 +281,39 @@
 
     def finish(s, i):
         v = streams[s, i] + links.total(i, s % 2)
-        if s < 2:
-            streams[s + 1, i] = v
-        else:
-            last[i] = v
+        streams[s + 1, i] = v
         normed[s + 1][i, core] = norm_rows(s + 1, v)
         links.gather((s, i), 2 * s + i, normed[s + 1].at[i])
 
+    def hits():
+        kept_choice = slots[...] < CAPACITY
+        index = jnp.where(kept_choice, routes[...] * SLOTS + slots[...], -1)
+        number = lax.broadcasted_iota(jnp.int32, (EXPERTS * SLOTS, rows_of), 0)
+        return [number == index[k : k + 1] for k in range(2)]
+
+    def make_pick():
+        first, second = hits()
+        flat = jnp.where(jnp.logical_or(first, second), 1.0, 0.0).astype(BF16)
+        pick[...] = dot_nt(flat, placement()).astype(BF16)
+
+    def make_spread():
+        first, second = hits()
+        flat = jnp.where(jnp.logical_or(first, second), 1.0, 0.0).astype(BF16)
+        spread[...] = dot_nt(placement(), flat).astype(BF16)
+
+    def make_gate():
+        gate[...] = sum(
+            jnp.sum(jnp.where(hit, gates[k : k + 1], 0.0), axis=1, keepdims=True)
+            for k, hit in enumerate(hits())
+        )
+
+    def make_cot():
+        cotp[...] = padded(cot)
+
+    def make_drow():
+        drow[...] = (dot(pick[...], cotp[...].reshape(2 * PAD, D)) * gate[...]).astype(BF16)
+
+    fill = (make_pick, make_spread, make_gate, make_cot, make_drow, None)
     steps = [(s, i) for s in range(3) for i in range(2)]
     for at, (s, i) in enumerate(steps):
         if s > 0:
@@ -228,14 +322,17 @@
         if at == 0:
             pl.semaphore_wait(barrier, 2)
         links.share(i, term)
+        if fill[at] is not None:
+            fill[at]()
         links.swap(i, s % 2)
         if at > 0:
             finish(*steps[at - 1])
+    for key in KEPT[:9]:
+        saves.start(key, kept[key], outs[key])
     finish(*steps[-1])
-
-    drow[...] = (dot(pick[...], cot[...].reshape(2 * PAD, D)) * gate[...]).astype(BF16)
-    for load in loads:
-        load.wait()
+    saves.start("streams", streams, outs["streams"])
+
+    loads.drain()
     for i in range(2):
         links.arrived((2, i))
     buf[...] = dot(pick[...], n3[...].reshape(2 * PAD, D)).astype(BF16)
@@ -247,47 +344,14 @@
         d = (slope * dot_nt(drow[cut], w_out[e])).astype(BF16)
         dhid[cut] = d
         dbuf[cut] = dot_nt(d, w_in[e]).astype(BF16)
-    for i in range(2):
-        links.share(i, dot(spread[i], dbuf[...]))
-    for i in range(2):
-        links.swap(i, 1)
-    for i in range(2):
-        links.share(2 + i, dot(spread[i], weighted[...]))
-    for i in range(2):
-        links.swap(2 + i, 1)
-    copies = []
-
-    def expert_grads(e):
-        cut = pl.ds(e * SLOTS, SLOTS)
         for m, left, right in ((e, buf, dhid), (EXPERTS + e, drow, eact)):
             weight_grad(ge, m, left[cut], right[cut])
-            copy = pltpu.make_async_copy(ge.at[m], ge_o.at[m], grad_sem.at[m])
-            copy.start()
-            copies.append(copy)
-
-    expert_grads(0)
-    expert_grads(1)
-    gains = biases = 0.0
-    for i in range(2):
-        dv, gain_term, bias_term = norm_back(last[i], gain[3:4], links.total(i, 1))
-        gains, biases = gains + gain_term, biases + bias_term
-        g = cot[i, core].astype(F32) + dv
-        g2[i] = g
-        du2[i, core] = g.astype(BF16)
-        links.gather((3, i), 6 + i, du2.at[i])
-    terms[...] = jnp.zeros_like(terms)
-    terms[3:4] = gains
-    terms[7:8] = biases
-    for i in range(2):
-        out_o[i, core] = last[i] + links.total(2 + i, 1)
-        links.gather((4, i), 8 + i, out_o.at[i])
-    expert_grads(2)
-    expert_grads(3)
-    for i in range(2):
-        links.arrived((3, i))
-        links.arrived((4, i))
-    for copy in copies:
-        copy.wait()
+            saves.start(("ge", m), ge.at[m], ge_o.at[m])
+    dn[...] = dot(spread[...], dbuf[...]).astype(BF16).reshape(2, 2, HALF, D)
+    saves.start("dn", dn, outs["dn"])
+    mo[...] = dot(spread[...], weighted[...]).astype(BF16).reshape(2, 2, HALF, D)
+    saves.start("mo", mo, outs["mo"])
+    saves.drain()
 
 
 class ImageSum:
@@ -371,20 +435,21 @@
         r = self.refs
         self.wait("b")
         own = self.block(0) if self.held else r["own"]
+        s1 = r["s1"] if self.held else own
 
         def add(m, carry):
             for b in range(4):
                 acc = own[m, b].astype(F32)
                 for k in range(2 if self.ring else 3):
                     acc = acc + r["rb"][k, m, b].astype(F32)
-                r["s1"][m, b] = acc.astype(BF16)
+                s1[m, b] = acc.astype(BF16)
             return carry
 
         lax.fori_loop(0, self.mats, add, 0)
         axis = "z" if self.order == "y" else "y"
         mine = self.place[1] if axis == "z" else self.place[0]
         for k in (2, 1, 3):
-            self.send("c", 5 + k, r["s1"].at[:, lax.rem(mine + k, 4)], r["rc"].at[k - 1], axis, k)
+            self.send("c", 5 + k, s1.at[:, lax.rem(mine + k, 4)], r["rc"].at[k - 1], axis, k)
 
     def third(self):
         r = self.refs
@@ -393,7 +458,7 @@
         self.wait("c")
         other = pl.ds(pl.multiple_of((1 - x) * 24, 8), 24)
         for m in range(self.mats):
-            acc = r["s1"][m, mine].astype(F32)
+            acc = r["s1" if self.held else "own"][m, mine].astype(F32)
             for k in range(3):
                 acc = acc + r["rc"][k, m].astype(F32)
             r["tot"][m] = acc
@@ -430,7 +495,7 @@
     pairs = (mats + 1) // 2
     shapes = {
         "rb": pltpu.VMEM((2 if ring else 3, mats, 4, 48, width), BF16),
-        "s1": pltpu.VMEM((mats, 4, 48, width), BF16),
+        "s1" if held else "own": pltpu.VMEM((mats, 4, 48, width), BF16),
         "rc": pltpu.VMEM((3, mats, 48, width), BF16),
         "tot": pltpu.VMEM((mats, 48, width), F32),
         "xs": pltpu.VMEM((pairs, 48, width), BF16),
@@ -439,27 +504,27 @@
     if ring:
         shapes["ra"] = pltpu.VMEM((2, mats, 4, 48, width // 2), BF16)
     if not held:
-        shapes["own"] = pltpu.VMEM((mats, 4, 48, width), BF16)
         shapes["near"] = pltpu.VMEM((2, mats, 4, 48, width // 2), BF16)
         shapes["local"] = pltpu.SemaphoreType.DMA((3,))
     return shapes
 
 
-BACK_IN = 18
-
-
 def backward_kernel(*refs):
+    hbm = dict(zip(KEPT, refs))
+    gain, ge, win_h, wout_h, m1_h, m2_h = refs[len(KEPT) : len(KEPT) + 6]
+    refs = refs[len(KEPT) + 6 :]
     (
-        n0, n1, n2, du2, qkv, att, probs, act, dgelu, streams, g2, terms,
-        gain, win, wout, m1, m2, ge,
-    ) = refs[:BACK_IN]
-    token_o, e_o, d_o, norm_o = refs[BACK_IN : BACK_IN + 4]
-    rest = list(refs[BACK_IN + 4 :])
+        out_o, token_o, gain_o, bias_o, heads_in_o, heads_out_o, m_in_o, m_out_o, e_in_o, e_out_o,
+    ) = refs[:10]
+    kept = dict(zip(KEPT, refs[10:]))
+    rest = refs[10 + len(KEPT) :]
     (
-        du1, du0, stack, dhid, g, gn, sums, sums_in, full, pair_out, pair_in, far_out, far_in,
-        send, recv, group_send, group_recv,
-    ) = rest[:17]
-    rest = rest[17:]
+        win, wout, m1, m2, outp, tokenp, g2, du2, du1, du0, stack, dhid, g, gn, sums, sums_in,
+        full, pair_out, pair_in, far_out, far_in,
+        send, recv, group_send, group_recv, load_sem,
+    ) = rest[:26]
+    rest = rest[26:]
+    n0, n1, n2, cotp, qkv, att, probs, act, dgelu, streams, dn, mo = (kept[k] for k in KEPT)
     links = TensorLinks((full, pair_out, pair_in, far_out, far_in), (send, recv))
     core = links.core
     dp = links.dp
@@ -467,23 +532,61 @@
     y, z, x = dp // 8, lax.rem(dp // 2, 4), lax.rem(dp, 2)
     place = (y, z, x, t)
 
-    def out_at(ref, base, cut):
-        def store(m, value):
-            ref[base + m, :, cut] = value
-
-        return store
-
-    everything = slice(None)
+    barrier = pltpu.get_barrier_semaphore()
+    for device in ((dp, links.other), (dp, links.far), (grid_device(y, z, 1 - x), t)):
+        pl.semaphore_signal(barrier, inc=1, device_id=device, device_id_type=MESH)
+    for k in (1, 2, 3):
+        for device in (grid_device(y + k, z, x), grid_device(y, z + k, x)):
+            pl.semaphore_signal(barrier, inc=1, device_id=(device, t), device_id_type=MESH)
+    loads = Loads(load_sem)
+    weights = {"win": (win_h, win), "wout": (wout_h, wout), "m1": (m1_h, m1), "m2": (m2_h, m2)}
+    order = (
+        "dn", "streams", "cotp", "mo", "wout", "qkv", "att", "probs", "win", "n2", "m2", "dgelu", "m1",
+        "n1", "act", "n0",
+    )
+    for key in order:
+        loads.start(key, *(weights[key] if key in weights else (hbm[key], kept[key])))
+
+    def store(ref, *index):
+        def put(m, value):
+            ref[index] = value
+
+        return put
+
+    def store_expert(ref):
+        def put(m, value):
+            ref[m] = value
+
+        return put
+
+    def store_heads(j, first):
+        def put(m, value):
+            width = heads_in_o.shape[-1]
+            low, high = value[:, :width], pltpu.roll(value, width, 1)[:, :width]
+            if first == 0:
+                heads_in_o[j, 0] = low
+                heads_in_o[j, 1] = high
+            else:
+                heads_in_o[j, 2] = low
+                heads_out_o[j] = high
+
+        return put
+
+    def store_norms(m, value):
+        turned = jnp.concatenate([value, jnp.zeros((104, 128), F32)], axis=0).T
+        gain_o[...] = turned[0:4, :24]
+        bias_o[...] = turned[4:8, :24]
+
     outs = {
-        "e0": out_at(e_o, 0, everything),
-        "e1": out_at(e_o, 4, everything),
-        "m0": out_at(d_o, 0, everything),
-        "m1": out_at(d_o, 1, everything),
-        "a1y": out_at(d_o, 3, slice(0, 384)),
-        "a1z": out_at(d_o, 3, slice(384, 768)),
-        "a0y": out_at(d_o, 2, slice(0, 384)),
-        "a0z": out_at(d_o, 2, slice(384, 768)),
-        "n": out_at(norm_o, 0, everything),
+        "e0": store_expert(e_in_o),
+        "e1": store_expert(e_out_o),
+        "m0": store(m_in_o, Ellipsis),
+        "m1": store(m_out_o, Ellipsis),
+        "a1y": store_heads(1, 0),
+        "a1z": store_heads(1, 384),
+        "a0y": store_heads(0, 0),
+        "a0z": store_heads(0, 384),
+        "n": store_norms,
     }
     groups = {}
     for at, (name, spec) in enumerate(GROUPS.items()):
@@ -492,17 +595,9 @@
         rest = rest[len(keys) :]
         groups[name] = ImageSum(spec, held, (group_send, group_recv), 10 * at, place, outs[name])
 
-    barrier = pltpu.get_barrier_semaphore()
-    for device in ((dp, links.other), (dp, links.far), (grid_device(y, z, 1 - x), t)):
-        pl.semaphore_signal(barrier, inc=1, device_id=device, device_id_type=MESH)
-    for k in (1, 2, 3):
-        for device in (grid_device(y + k, z, x), grid_device(y, z + k, x)):
-            pl.semaphore_signal(barrier, inc=1, device_id=(device, t), device_id_type=MESH)
     pl.semaphore_wait(barrier, 9)
-
     groups["e0"].start(ge.at[0:4])
     groups["e1"].start(ge.at[4:8])
-    sums[...] = terms[...]
 
     def rows(ref, i):
         return ref[i].reshape(PAD, D)
@@ -514,87 +609,117 @@
         links.share(i, value)
         links.swap(i, parity)
 
-    def finish(s, parity, i, target, slot):
+    def finish(s, parity, i, base, target, slot):
         dv, gain_term, bias_term = norm_back(streams[s, i], gain[s : s + 1], links.total(i, parity))
         sums[s : s + 1] = sums[s : s + 1] + gain_term
         sums[4 + s : 5 + s] = sums[4 + s : 5 + s] + bias_term
-        v = g2[i] + dv
+        v = base[i].astype(F32) + dv if s < 3 else base[i, core].astype(F32) + dv
         if s > 0:
             g2[i] = v
             target[i, core] = v.astype(BF16)
         else:
             target[i, core] = v
-        links.gather((s, i), 2 * s + slot, target.at[i])
-
-    for i in range(2):
+        links.gather((s, i), 2 * slot + i, target.at[i])
+
+    def write_rows(ref, pad):
+        for i in range(2):
+            ref[i * SEQ : (i + 1) * SEQ] = pad[i].reshape(PAD, D)[:SEQ]
+
+    sums[...] = jnp.zeros_like(sums)
+    loads.need("dn")
+    for i in range(2):
+        links.share_held(i, dn.at[i])
+    for i in range(2):
+        links.swap(i, 1)
+    loads.need("mo")
+    for i in range(2):
+        links.share_held(2 + i, mo.at[i])
+    loads.need("streams", "cotp")
+    for i in range(2):
+        finish(3, 1, i, cotp, du2, 0)
+    for i in range(2):
+        links.swap(2 + i, 0)
+
+    loads.need("wout", "qkv", "att", "probs", "win")
+    for i in range(2):
+        links.arrived((3, i))
         share(0, i, attention_backward(rows(du2, i), win, wout, 1, i, qkv, att, probs, stack))
+    loads.need("n2")
     head_grad(g, 3, flat(n2), flat(du2), stack)
     groups["a1y"].start(g.at[3:4, :, :, :, 0:384])
     groups["a1z"].start(g.at[3:4, :, :, :, 384:768])
     for i in range(2):
-        finish(2, 0, i, du1, i)
-
+        finish(2, 0, i, g2, du1, 1)
+    for i in range(2):
+        outp[i, core] = streams[3, i] + links.total(2 + i, 0)
+        links.gather((4, i), 8 + i, outp.at[i])
+
+    loads.need("m2", "dgelu", "m1")
     for i in range(2):
         links.arrived((2, i))
         d = (dgelu[i] * dot_nt(rows(du1, i), m2[...])).astype(BF16)
         dhid[i] = d
         share(1, i, dot_nt(d, m1[...]))
+    groups["e0"].middle()
+    groups["e1"].middle()
+    loads.need("n1", "act")
     weight_grad(g, 0, flat(n1), dhid[...].reshape(2 * PAD, D))
     groups["m0"].start(g.at[0:1])
     weight_grad(g, 1, flat(du1), act[...].reshape(2 * PAD, D))
     groups["m1"].start(g.at[1:2])
     for i in range(2):
-        finish(1, 1, i, du0, i)
+        finish(1, 1, i, g2, du0, 2)
 
     for i in range(2):
         links.arrived((1, i))
         share(0, i, attention_backward(rows(du0, i), win, wout, 0, i, qkv, att, probs, stack))
-    groups["e0"].middle()
-    groups["e1"].middle()
+    loads.need("n0")
     head_grad(g, 2, flat(n0), flat(du0), stack)
     groups["a0y"].start(g.at[2:3, :, :, :, 0:384])
     groups["a0z"].start(g.at[2:3, :, :, :, 384:768])
     for i in range(2):
-        finish(0, 0, i, token_o, i)
-    both = links.copy(sums, sums_in, 18, links.other)
-    groups["a1y"].second()
-    groups["a1z"].second()
-    groups["m0"].middle()
-    groups["m1"].middle()
+        finish(0, 0, i, g2, tokenp, 3)
+    both = links.copy(sums, sums_in, 20, links.other)
+    for i in range(2):
+        links.arrived((4, i))
+    write_rows(out_o, outp)
     both.wait()
     wide = jnp.concatenate([sums[...] + sums_in[...], jnp.zeros((120, D), F32)], axis=0)
     gn[0] = wide.T.astype(BF16).reshape(4, 4, 48, 128)
     groups["n"].start(gn)
-    for name in ("e0", "e1", "a0y", "a0z", "m0", "m1", "n"):
+    for name in ("m0", "m1"):
+        groups[name].middle()
+    for name in ("e0", "e1", "a1y", "a1z", "a0y", "a0z", "n", "m0", "m1"):
         groups[name].second()
-    for name in ("a1y", "a1z", "e0", "e1", "a0y", "a0z", "m0", "m1", "n"):
+    for i in range(2):
+        links.arrived((0, i))
+    write_rows(token_o, tokenp)
+    for name in ("e0", "e1", "a1y", "a1z", "a0y", "a0z", "n", "m0", "m1"):
         groups[name].third()
-    for name in ("a1y", "a1z", "e0", "e1", "a0y", "a0z", "m0", "m1", "n"):
+    for name in ("e0", "e1", "a1y", "a1z", "a0y", "a0z", "n", "m0", "m1"):
         groups[name].finish()
-    for i in range(2):
-        links.arrived((0, i))
+
+
+def publish_kernel(*refs):
+    count = len(refs) // 2
+    sems = refs[-1]
+    copies = [pltpu.make_async_copy(refs[k], refs[count + k], sems.at[k]) for k in range(count)]
+    for copy in copies:
+        copy.start()
+    for copy in copies:
+        copy.wait()
 
 
 def link_scratch(channels, sems):
     return [
-        pltpu.VMEM((channels, 2, HALF, D), F32),
+        pltpu.VMEM((2, 2, HALF, D), F32),
+        pltpu.VMEM((2, HALF, D), BF16),
         pltpu.VMEM((channels, HALF, D), BF16),
         pltpu.VMEM((channels, HALF, D), BF16),
-        pltpu.VMEM((channels, HALF, D), BF16),
-        pltpu.VMEM((2, channels, HALF, D), BF16),
+        pltpu.VMEM((2 + channels, HALF, D), BF16),
         pltpu.SemaphoreType.DMA((sems,)),
         pltpu.SemaphoreType.DMA((sems,)),
     ]
-
-
-def padded(v):
-    v = v.reshape(2, SEQ, -1)
-    v = jnp.pad(v, ((0, 0), (0, PAD - SEQ), (0, 0)))
-    return v.reshape(2, 2, HALF, v.shape[-1])
-
-
-def unpadded(v):
-    return v.reshape(2, PAD, D)[:, :SEQ].reshape(2 * SEQ, D)
 
 
 def local(
@@ -613,70 +738,58 @@
     cotangent,
 ):
     head_width = attn_out.shape[1]
-    kept = slot_index < CAPACITY
-    index = jnp.where(kept, routes * SLOTS + slot_index, -1)
-    index = jnp.pad(index.reshape(2, SEQ, 2), ((0, 0), (0, PAD - SEQ), (0, 0)), constant_values=-1)
-    gates = jnp.pad(gate_weights.reshape(2, SEQ, 2), ((0, 0), (0, PAD - SEQ), (0, 0)))
     slots = EXPERTS * SLOTS
-    flat = index.reshape(2 * PAD, 2)
-    number = lax.broadcasted_iota(jnp.int32, (slots, 2 * PAD), 0)
-    hits = [number == flat[:, k][None, :] for k in range(2)]
-    pick = jnp.logical_or(*hits).astype(BF16)
-    gate = sum(
-        jnp.sum(jnp.where(hits[k], gates.reshape(2 * PAD, 2)[:, k][None, :], 0.0), axis=1, keepdims=True)
-        for k in range(2)
-    )
-    number = lax.broadcasted_iota(jnp.int32, (2, PAD, slots), 2)
-    spread = jnp.logical_or(number == index[:, :, :1], number == index[:, :, 1:]).astype(BF16)
-
+    rows = tokens.shape[0]
     whole = pl.BlockSpec(memory_space=pltpu.VMEM)
     hbm = pl.BlockSpec(memory_space=pl.ANY)
     shape = jax.ShapeDtypeStruct
     half_rows = (2, 2, HALF, D)
-    win = attn_in.reshape(6, D, head_width)
-    (out, n0, n1, n2, du2, qkv, att, probs, act, dgelu, streams, g2, terms, ge) = pl.pallas_call(
+    win = jnp.swapaxes(attn_in, 2, 3).reshape(6, head_width, D)
+    kept = kept_shapes(head_width)
+    keeping = [pltpu.VMEM(*kept[key]) for key in KEPT]
+    grads = pltpu.VMEM((2 * EXPERTS, 4, 4, 48, D), BF16)
+    *stored, ge = pl.pallas_call(
         forward_kernel,
-        out_shape=[
-            shape(half_rows, F32),
-            shape(half_rows, BF16),
-            shape(half_rows, BF16),
-            shape(half_rows, BF16),
-            shape(half_rows, BF16),
-            shape((2, 3, 2, PAD, head_width), BF16),
-            shape((2, 2, PAD, head_width), BF16),
-            shape((2, 2, 3, PAD, PAD), F32),
-            shape((2, PAD, D), BF16),
-            shape((2, PAD, D), F32),
-            shape((3, 2, HALF, D), F32),
-            shape((2, HALF, D), F32),
-            shape((8, D), F32),
-            shape((2 * EXPERTS, 4, 4, 48, D), BF16),
-        ],
-        in_specs=[whole] * 11 + [hbm] * 2,
-        out_specs=[whole] * 13 + [hbm],
-        scratch_shapes=[
+        out_shape=[shape(*kept[key]) for key in KEPT] + [shape(grads.shape, BF16)],
+        in_specs=[whole] * 9 + [hbm] * 4,
+        out_specs=[hbm] * (len(KEPT) + 1),
+        scratch_shapes=keeping
+        + [
             pltpu.VMEM(half_rows, BF16),
-            pltpu.VMEM((2, HALF, D), F32),
+            pltpu.VMEM((slots, 2 * PAD), BF16),
+            pltpu.VMEM((2 * PAD, slots), BF16),
+            pltpu.VMEM((slots, 1), F32),
         ]
         + [pltpu.VMEM((slots, D), BF16)] * 6
         + [
+            pltpu.VMEM((D, D), BF16),
+            pltpu.VMEM((D, D), BF16),
             pltpu.VMEM((EXPERTS, D, D), BF16),
             pltpu.VMEM((EXPERTS, D, D), BF16),
-            pltpu.VMEM((2 * EXPERTS, 4, 4, 48, D), BF16),
+            grads,
         ]
-        + link_scratch(4, 22)
-        + [pltpu.SemaphoreType.DMA((8,)), pltpu.SemaphoreType.DMA((8,))],
+        + link_scratch(2, 18)
+        + [pltpu.SemaphoreType.DMA((10,)), pltpu.SemaphoreType.DMA((20,))],
         compiler_params=pltpu.CompilerParams(
             collective_id=1, has_side_effects=True, vmem_limit_bytes=60 << 20
         ),
         name="forward",
     )(
-        padded(tokens), padded(cotangent), norm_gain, norm_bias, win, attn_out, mlp_in, mlp_out,
-        pick, spread, gate, expert_in, expert_out,
+        tokens, cotangent, routes.T, slot_index.T, gate_weights.T, norm_gain, norm_bias, win, attn_out,
+        mlp_in, mlp_out, expert_in, expert_out,
     )
 
     scratch = (
-        [
+        keeping
+        + [
+            pltpu.VMEM((6, head_width, D), BF16),
+            pltpu.VMEM((2, head_width, D), BF16),
+            pltpu.VMEM((D, D), BF16),
+            pltpu.VMEM((D, D), BF16),
+            pltpu.VMEM(half_rows, F32),
+            pltpu.VMEM(half_rows, F32),
+            pltpu.VMEM((2, HALF, D), F32),
+            pltpu.VMEM(half_rows, BF16),
             pltpu.VMEM(half_rows, BF16),
             pltpu.VMEM(half_rows, BF16),
             pltpu.VMEM((2 * PAD, D), BF16),
@@ -686,48 +799,56 @@
             pltpu.VMEM((8, D), F32),
             pltpu.VMEM((8, D), F32),
         ]
-        + link_scratch(2, 20)
+        + link_scratch(4, 22)
         + [
             pltpu.SemaphoreType.DMA((10 * len(GROUPS),)),
             pltpu.SemaphoreType.DMA((10 * len(GROUPS),)),
+            pltpu.SemaphoreType.DMA((16,)),
         ]
     )
     for spec in GROUPS.values():
         scratch += list(group_scratch(spec).values())
-    token_grad, experts, dense, norms = pl.pallas_call(
+    results = pl.pallas_call(
         backward_kernel,
         out_shape=[
-            shape(half_rows, F32),
-            shape((2 * EXPERTS, 24, D), F32),
-            shape((4, 24, D), F32),
-            shape((1, 24, 128), F32),
+            shape((rows, D), F32),
+            shape((rows, D), F32),
+            shape((4, 24), F32),
+            shape((4, 24), F32),
+            shape((2, 3, 24, head_width), F32),
+            shape((2, 24, head_width), F32),
+            shape((24, D), F32),
+            shape((24, D), F32),
+            shape((EXPERTS, 24, D), F32),
+            shape((EXPERTS, 24, D), F32),
         ],
-        in_specs=[whole] * (BACK_IN - 1) + [hbm],
-        out_specs=[whole] * 4,
+        in_specs=[hbm] * len(KEPT) + [whole] + [hbm] * 5,
+        out_specs=[whole] * 10,
         scratch_shapes=scratch,
         compiler_params=pltpu.CompilerParams(
-            collective_id=2, has_side_effects=True, vmem_limit_bytes=60 << 20
+            collective_id=2, has_side_effects=True, vmem_limit_bytes=62 << 20
         ),
         name="backward",
-    )(
-        n0, n1, n2, du2, qkv, att, probs, act, dgelu, streams, g2, terms,
-        norm_gain, win, attn_out, mlp_in, mlp_out, ge,
-    )
-    heads = dense[2:]
-    attn_in_sum = jnp.stack(
-        [heads[:, :, c * head_width : (c + 1) * head_width] for c in range(3)], axis=1
-    )
+    )(*stored, norm_gain, ge, win, attn_out, mlp_in, mlp_out)
+    out, token_grad, gains, biases, heads_in, heads_out, m_in, m_out, e_in, e_out = pl.pallas_call(
+        publish_kernel,
+        out_shape=[shape(r.shape, r.dtype) for r in results],
+        in_specs=[hbm] * len(results),
+        out_specs=[whole] * len(results),
+        scratch_shapes=[pltpu.SemaphoreType.DMA((len(results),))],
+        name="publish",
+    )(*results)
     return (
-        unpadded(out),
-        unpadded(token_grad),
-        norms[0, :, :4].T,
-        norms[0, :, 4:8].T,
-        attn_in_sum,
-        jnp.swapaxes(heads[:, :, 3 * head_width :], 1, 2),
-        dense[0],
-        dense[1].T,
-        experts[:EXPERTS],
-        jnp.swapaxes(experts[EXPERTS:], 1, 2),
+        out,
+        token_grad,
+        gains,
+        biases,
+        heads_in,
+        jnp.swapaxes(heads_out, 1, 2),
+        m_in,
+        m_out.T,
+        e_in,
+        jnp.swapaxes(e_out, 1, 2),
     )
 
 

time: 197 us -> 159 us (0.81)
  Pallas kernels: 177 us -> 158 us
  local copies, waits for them, and re-layouts: 14.9 us -> 0 us
  other arithmetic: 3.45 us -> 0 us
    pallas_call x2 -> x3, Pallas kernels: 177 us -> 158 us  [the longest x1 103 us: local(): pl.pallas_call(backward_kernel, out_shape=[shape((rows, D), F32), shape((...]
    reshape x8 -> x0, local copies, waits for them, and re-layouts: 4.66 us -> none  [the longest x2 2.3 us: unpadded(): return v.reshape(2, PAD, D)[:, :SEQ].reshape(2 * SEQ, D)]
    unnamed x16 -> x0, local copies, waits for them, and re-layouts: 3.79 us -> none
    convert_element_type x2 -> x0, other arithmetic: 2.3 us -> none  [the longest x1 1.2 us: local(): pick = jnp.logical_or(*hits).astype(BF16)]
    transpose x3 -> x0, local copies, waits for them, and re-layouts: 2.21 us -> none  [the longest x1 0.85 us: local(): jnp.swapaxes(experts[EXPERTS:], 1, 2)]
where the time goes in v3:
time: 159 us
  Pallas kernels  158 us (99%)
    pallas_call x1, Pallas kernels, local(): pl.pallas_call(backward_kernel, out_shape=[shape((rows, D), F32), shape((...  103 us
    pallas_call x1, Pallas kernels, local(): pl.pallas_call(forward_kernel, out_shape=[shape(*kept[key]) for key in KE...  50.9 us
    pallas_call x1, Pallas kernels, local(): pl.pallas_call(publish_kernel, out_shape=[shape(r.shape, r.dtype) for r i...  3.74 us

profile of v3, /device:TPU:0, one launch (start us, length us, event | category | flops | bytes accessed | tf_op | source)
XLA Modules:
  0.0 158.7 jit_solution(1291454165166280035)
XLA Ops:
  0.6 50.9 %forward.1 = (bf16[2,2,112,768]{3,2,1,0:T(8,128)(2,1)}, bf16[2,2,112,768]{3,2,1,0:T(8,128)(2,1)}, bf16[2,2,112,768]{3,2,1,0:T(8,128)(2,1)}, bf16[2,2,112,768]{3,...) custom-call(bf16[394,768]{1,0:T(8,128)(2,1)} %tokens.1, ...), custom_call_target="tpu_custom_call" | custom-call | tf_op jit(solution)/shard_map/forward/pallas_call | solution.py:751
  51.6 103.2 %backward.1 = (f32[394,768]{1,0:T(8,128)}, f32[394,768]{1,0:T(8,128)}, f32[4,24]{1,0:T(4,128)}, f32[4,24]{1,0:T(4,128)}, f32[2,3,24,192]{3,2,1,0:T(8,128)}, /*in...) custom-call(bf16[2,2,112,768]{3,2,1,0:T(8,128)(2,1)} %get-tuple-elem, ...), custom_call_target="tpu_custom_call" | custom-call | tf_op jit(solution)/shard_map/backward/pallas_call | solution.py:811
  154.8 3.7 %publish.1 = (f32[394,768]{1,0:T(8,128)}, f32[394,768]{1,0:T(8,128)}, f32[4,24]{1,0:T(4,128)}, f32[4,24]{1,0:T(4,128)}, f32[2,3,24,192]{3,2,1,0:T(8,128)}, /*ind...) custom-call(f32[394,768]{1,0:T(8,128)} %get-tuple-element.56.refs_0_, ...), custom_call_target="tpu_custom_call" | custom-call | tf_op jit(solution)/shard_map/publish/pallas_call | solution.py:833

commit v4 on v3

v4 whole, which is shorter than its diff:
```python
import functools

import jax
import jax.numpy as jnp
from jax import lax
from jax.experimental import pallas as pl
from jax.experimental.pallas import tpu as pltpu
from jax.sharding import PartitionSpec as P

D = 768
HEAD_DIM = 64
SEQ = 197
HALF = 112
PAD = 2 * HALF
CAPACITY = 168
SLOTS = 176
EXPERTS = 4
NORM_EPSILON = 1e-06
MESH = pl.DeviceIdType.MESH
F32 = jnp.float32
BF16 = jnp.bfloat16


def dot(a, b):
    return lax.dot_general(a, b, (((1,), (0,)), ((), ())), preferred_element_type=F32)


def dot_nt(a, b):
    return lax.dot_general(a, b, (((1,), (1,)), ((), ())), preferred_element_type=F32)


def dot_tn(a, b):
    return lax.dot_general(a, b, (((0,), (0,)), ((), ())), preferred_element_type=F32)


def grid_device(y, z, x):
    return (lax.rem(y + 8, 4) * 4 + lax.rem(z + 8, 4)) * 2 + x


def normalize(v):
    center = v - jnp.mean(v, axis=-1, keepdims=True)
    spread = jnp.mean(center * center, axis=-1, keepdims=True)
    scale = lax.rsqrt(spread + NORM_EPSILON)
    return center * scale, scale


def norm_back(v, gain_row, upstream):
    nhat, scale = normalize(v)
    scaled = upstream * gain_row
    mean = jnp.mean(scaled, axis=-1, keepdims=True)
    along = jnp.mean(scaled * nhat, axis=-1, keepdims=True)
    dv = (scaled - mean - nhat * along) * scale
    gain_term = jnp.sum(upstream * nhat, axis=0, keepdims=True)
    bias_term = jnp.sum(upstream, axis=0, keepdims=True)
    return dv, gain_term, bias_term


def gelu_pair(h):
    phi = 0.5 * (1.0 + lax.erf(h * 0.7071067811865476))
    density = jnp.exp(-0.5 * h * h) * 0.3989422804014327
    return (h * phi).astype(BF16), phi + h * density


def head_mask(h, width):
    lane = lax.broadcasted_iota(jnp.int32, (1, width), 1)
    return jnp.logical_and(lane >= h * HEAD_DIM, lane < (h + 1) * HEAD_DIM)


def only(h, v):
    return jnp.where(head_mask(h, v.shape[1]), v, jnp.zeros((), v.dtype))


class TensorLinks:
    def __init__(self, refs, sems):
        self.own, self.pair_out, self.pair_in, self.far_out, self.far_in = refs
        self.sems = sems
        self.dp = lax.axis_index("dp")
        t = lax.axis_index("tensor")
        self.core = lax.rem(t, 2)
        self.other = t + 1 - 2 * self.core
        self.far = lax.rem(t + 2, 4)
        self.pairs, self.fars, self.gathers, self.mine = {}, {}, {}, {}

    def copy(self, source, target, slot, device):
        send, recv = self.sems
        c = pltpu.make_async_remote_copy(
            src_ref=source,
            dst_ref=target,
            send_sem=send.at[slot],
            recv_sem=recv.at[slot],
            device_id=(self.dp, device),
            device_id_type=MESH,
        )
        c.start()
        return c

    def share(self, ch, value):
        low, high = value[:HALF], value[HALF:]
        self.pair_out[ch] = jnp.where(self.core == 0, high, low).astype(BF16)
        self.pairs[ch] = self.copy(self.pair_out.at[ch], self.pair_in.at[ch], ch, self.other)
        self.own[ch] = jnp.where(self.core == 0, low, high)
        self.mine[ch] = lambda: self.own[ch]

    def share_held(self, ch, ref):
        self.pairs[ch] = self.copy(ref.at[1 - self.core], self.pair_in.at[ch], ch, self.other)
        self.mine[ch] = lambda: ref[self.core].astype(F32)

    def place(self, ch, parity):
        return 2 * parity + ch if ch < 2 else 2 + ch

    def swap(self, ch, parity):
        self.pairs.pop(ch).wait()
        mine = self.mine.pop(ch)() + self.pair_in[ch].astype(F32)
        self.far_out[ch] = mine.astype(BF16)
        at = self.place(ch, parity)
        self.fars[ch] = self.copy(self.far_out.at[ch], self.far_in.at[at], 4 + at, self.far)

    def total(self, ch, parity):
        self.fars.pop(ch).wait()
        return self.far_out[ch].astype(F32) + self.far_in[self.place(ch, parity)].astype(F32)

    def gather(self, key, slot, ref):
        half = ref.at[self.core]
        self.gathers[key] = self.copy(half, half, 10 + slot, self.other)

    def arrived(self, key):
        self.gathers.pop(key).wait()


class Loads:
    def __init__(self, sems):
        self.sems, self.pending, self.count = sems, {}, 0

    def start(self, key, source, target):
        c = pltpu.make_async_copy(source, target, self.sems.at[self.count])
        c.start()
        self.count += 1
        self.pending[key] = c

    def need(self, *keys):
        for key in keys:
            if key in self.pending:
                self.pending.pop(key).wait()

    def drain(self):
        self.need(*list(self.pending))


def attention_forward(n, win, wout, j, i, qkv, att, probs):
    q, k, v = (dot_nt(n, win[3 * j + c]).astype(BF16) for c in range(3))
    for c, part in enumerate((q, k, v)):
        qkv[j, c, i] = part
    key = lax.broadcasted_iota(jnp.int32, (1, PAD), 1)
    mixed = None
    for h in range(3):
        s = dot_nt(only(h, q), k) * 0.125
        s = jnp.where(key < SEQ, s, -1e30)
        e = jnp.exp(s - jnp.max(s, axis=-1, keepdims=True))
        p = e * (1.0 / jnp.sum(e, axis=-1, keepdims=True))
        p = p.astype(BF16)
        probs[j, i, h] = p
        term = dot(p, only(h, v))
        mixed = term if mixed is None else mixed + term
    mixed = mixed.astype(BF16)
    att[j, i] = mixed
    return dot(mixed, wout[j])


def attention_backward(du, win, wout, j, i, qkv, att, probs, stack):
    q, k, v = (qkv[j, c, i] for c in range(3))
    d_att = dot_nt(du, wout[j]).astype(BF16)
    dq = dk = dv = None
    for h in range(3):
        low = probs[j, i, h]
        p = low.astype(F32)
        dp = dot_nt(only(h, d_att), v)
        ds = (p * (dp - jnp.sum(p * dp, axis=-1, keepdims=True))).astype(BF16)
        terms = (dot(ds, only(h, k)), dot_tn(ds, only(h, q)), dot_tn(low, only(h, d_att)))
        dq, dk, dv = terms if dq is None else (a + b for a, b in zip((dq, dk, dv), terms))
    parts = [(dq * 0.125).astype(BF16), (dk * 0.125).astype(BF16), dv.astype(BF16)]
    stack[i * PAD : (i + 1) * PAD] = jnp.concatenate(parts + [att[j, i]], axis=1)
    return sum(dot(part, win[3 * j + c]) for c, part in enumerate(parts))


def weight_grad(g, m, left, right):
    for s in range(2):
        out = dot_tn(left[:, s * 384 : (s + 1) * 384], right).astype(BF16)
        g[m, 2 * s : 2 * s + 2] = out.reshape(2, 4, 48, D)


def head_grad(g, m, n, du, stack):
    lane = lax.broadcasted_iota(jnp.int32, (1, 256), 1)
    last = stack[:, 512:]
    zero = jnp.zeros((), BF16)
    for s in range(2):
        cut = slice(s * 384, (s + 1) * 384)
        a = dot_tn(n[:, cut], stack[:, :512]).astype(BF16)
        b = dot_tn(n[:, cut], jnp.where(lane < 64, last, zero))
        b = (b + dot_tn(du[:, cut], jnp.where(lane < 64, zero, last))).astype(BF16)
        g[m, 2 * s : 2 * s + 2, :, :, 0:512] = a.reshape(2, 4, 48, 512)
        g[m, 2 * s : 2 * s + 2, :, :, 512:] = b.reshape(2, 4, 48, 256)


class ImageSum:
    def __init__(self, spec, refs, sems, base, place, out):
        self.mats, self.width, self.order, self.ring = spec
        self.refs, self.sems, self.base, self.place, self.out = refs, sems, base, place, out
        self.copies = {}

    def send(self, name, slot, source, target, axis, k):
        y, z, x, t = self.place
        if axis == "x":
            device = grid_device(y, z, 1 - x)
        else:
            device = grid_device(y + k, z, x) if axis == "y" else grid_device(y, z + k, x)
        send, recv = self.sems
        c = pltpu.make_async_remote_copy(
            src_ref=source,
            dst_ref=target,
            send_sem=send.at[self.base + slot],
            recv_sem=recv.at[self.base + slot],
            device_id=(device, t),
            device_id_type=MESH,
        )
        c.start()
        self.copies.setdefault(name, []).append(c)

    def wait(self, name):
        for c in self.copies.pop(name, []):
            c.wait()

    def block(self, k):
        source, y, z = self.source, self.place[0], self.place[1]
        if self.order == "y":
            return source.at[:, lax.rem(y + k, 4)]
        return source.at[:, :, lax.rem(z + k, 4)]

    def start(self, source):
        self.source = source
        axis, h = self.order, self.width // 2
        r = self.refs
        low, high = pl.ds(0, h), pl.ds(h, h)
        if self.ring:
            far = self.block(2)
            self.send("a", 0, far.at[:, :, :, low], r["ra"].at[0], axis, 1)
            self.send("a", 1, far.at[:, :, :, high], r["ra"].at[1], axis, 3)
            self.send("b", 2, self.block(1).at[:, :, :, high], r["rb"].at[0, :, :, :, high], axis, 1)
            self.send("b", 3, self.block(3).at[:, :, :, low], r["rb"].at[1, :, :, :, low], axis, 3)
        else:
            for k in (2, 1, 3):
                self.send("b", k, self.block(k), r["rb"].at[k - 1], axis, k)

    def middle(self):
        r, h = self.refs, self.width // 2
        low, high = pl.ds(0, h), pl.ds(h, h)
        self.wait("a")
        for side, k, cut in ((0, 1, low), (1, 3, high)):
            near = self.block(k).at[:, :, :, cut]

            def add(m, carry, near=near, side=side):
                for b in range(4):
                    r["ra"][side, m, b] = (r["ra"][side, m, b].astype(F32) + near[m, b].astype(F32)).astype(BF16)
                return carry

            lax.fori_loop(0, self.mats, add, 0)
        self.send("b", 4, r["ra"].at[0], r["rb"].at[0, :, :, :, low], self.order, 1)
        self.send("b", 5, r["ra"].at[1], r["rb"].at[1, :, :, :, high], self.order, 3)

    def second(self):
        r = self.refs
        self.wait("b")
        own = s1 = self.block(0)

        def add(m, carry):
            for b in range(4):
                acc = own[m, b].astype(F32)
                for k in range(2 if self.ring else 3):
                    acc = acc + r["rb"][k, m, b].astype(F32)
                s1[m, b] = acc.astype(BF16)
            return carry

        lax.fori_loop(0, self.mats, add, 0)
        axis = "z" if self.order == "y" else "y"
        mine = self.place[1] if axis == "z" else self.place[0]
        for k in (2, 1, 3):
            self.send("c", 5 + k, s1.at[:, lax.rem(mine + k, 4)], r["rc"].at[k - 1], axis, k)

    def total(self, m):
        r = self.refs
        y, z, x, t = self.place
        acc = self.block(0)[m, z if self.order == "y" else y].astype(F32)
        for k in range(3):
            acc = acc + r["rc"][k, m].astype(F32)
        return acc

    def third(self):
        r = self.refs
        x = self.place[2]
        self.wait("c")
        for m in range(0, self.mats, 2):
            pieces = [self.total(n) for n in (m, min(m + 1, self.mats - 1))]
            pieces = [jnp.where(x == 0, v[24:], v[:24]) for v in pieces]
            r["xs"][m // 2] = jnp.concatenate(pieces, axis=0).astype(BF16)
        self.send("d", 9, r["xs"], r["xr"], "x", 0)

    def finish(self):
        r = self.refs
        x = self.place[2]
        self.wait("d")
        for m in range(self.mats):
            theirs = r["xr"][m // 2].astype(F32)
            v = self.total(m)
            mine = jnp.where(x == 0, v[:24], v[24:])
            self.out(m, mine + theirs[24 * (m % 2) : 24 * (m % 2) + 24])


GROUPS = {
    "eay": (2, 768, "y", True),
    "eaz": (2, 768, "z", True),
    "eby": (2, 768, "y", True),
    "ebz": (2, 768, "z", True),
    "m0": (1, 768, "y", True),
    "m1": (1, 768, "z", True),
    "a1y": (1, 384, "y", False),
    "a1z": (1, 384, "z", False),
    "a0y": (1, 384, "y", False),
    "a0z": (1, 384, "z", False),
    "n": (1, 128, "y", False),
}


def group_scratch(spec):
    mats, width, order, ring = spec
    pairs = (mats + 1) // 2
    shapes = {
        "rb": pltpu.VMEM((2 if ring else 3, mats, 4, 48, width), BF16),
        "rc": pltpu.VMEM((3, mats, 48, width), BF16),
        "xs": pltpu.VMEM((pairs, 48, width), BF16),
        "xr": pltpu.VMEM((pairs, 48, width), BF16),
    }
    if ring:
        shapes["ra"] = pltpu.VMEM((2, mats, 4, 48, width // 2), BF16)
    return shapes


def layers_kernel(
    tokens, cot, routes, slots, gates, gain, bias, win, wout, m1_h, m2_h, ein, eout, *refs
):
    (
        out_o, token_o, gain_o, bias_o, heads_in_o, heads_out_o, m_in_o, m_out_o, e_in_o, e_out_o,
    ) = refs[:10]
    (
        n0, n1, n2, n3, du2, du1, du0, qkv, att, probs, act, dgelu, streams, g2,
        pick, spread, gate, buf, drow, weighted, dbuf, m1, m2, g, ge, gn, sums, sums_in,
        own, pair_out, pair_in, far_out, far_in,
        send, recv, group_send, group_recv, load_sem,
    ) = refs[10:48]
    rest = refs[48:]
    dn, mo, cotp = n3, du0, du1
    stack = weighted.at[0 : 2 * PAD]
    dhid = dbuf
    links = TensorLinks((own, pair_out, pair_in, far_out, far_in), (send, recv))
    core = links.core
    dp = links.dp
    t = lax.axis_index("tensor")
    y, z, x = dp // 8, lax.rem(dp // 2, 4), lax.rem(dp, 2)
    place = (y, z, x, t)

    barrier = pltpu.get_barrier_semaphore()
    for device in ((dp, links.other), (dp, links.far), (grid_device(y, z, 1 - x), t)):
        pl.semaphore_signal(barrier, inc=1, device_id=device, device_id_type=MESH)
    for k in (1, 2, 3):
        for device in (grid_device(y + k, z, x), grid_device(y, z + k, x)):
            pl.semaphore_signal(barrier, inc=1, device_id=(device, t), device_id_type=MESH)

    def store(ref, *index):
        def put(m, value):
            ref[index] = value

        return put

    def store_expert(ref, base):
        def put(m, value):
            ref[base + m] = value

        return put

    def store_heads(j, first):
        def put(m, value):
            width = heads_in_o.shape[-1]
            low, high = value[:, :width], pltpu.roll(value, width, 1)[:, :width]
            if first == 0:
                heads_in_o[j, 0] = low
                heads_in_o[j, 1] = high
            else:
                heads_in_o[j, 2] = low
                heads_out_o[j] = high

        return put

    def store_norms(m, value):
        turned = jnp.concatenate([value, jnp.zeros((104, 128), F32)], axis=0).T
        gain_o[...] = turned[0:4, :24]
        bias_o[...] = turned[4:8, :24]

    outs = {
        "eay": store_expert(e_in_o, 0),
        "eaz": store_expert(e_out_o, 0),
        "eby": store_expert(e_in_o, 2),
        "ebz": store_expert(e_out_o, 2),
        "m0": store(m_in_o, Ellipsis),
        "m1": store(m_out_o, Ellipsis),
        "a1y": store_heads(1, 0),
        "a1z": store_heads(1, 384),
        "a0y": store_heads(0, 0),
        "a0z": store_heads(0, 384),
        "n": store_norms,
    }
    groups = {}
    for at, (name, spec) in enumerate(GROUPS.items()):
        keys = list(group_scratch(spec))
        held = dict(zip(keys, rest[: len(keys)]))
        rest = rest[len(keys) :]
        groups[name] = ImageSum(spec, held, (group_send, group_recv), 10 * at, place, outs[name])

    loads = Loads(load_sem)
    loads.start("m1", m1_h, m1)
    loads.start("m2", m2_h, m2)

    def fetch(e):
        loads.start(("in", e), ein.at[e], g.at[2 * (e % 2)])
        loads.start(("out", e), eout.at[e], g.at[2 * (e % 2) + 1])

    fetch(0)
    fetch(1)
    rows_of = tokens.shape[0]

    def placement():
        row = lax.broadcasted_iota(jnp.int32, (2 * PAD, rows_of), 0)
        column = lax.broadcasted_iota(jnp.int32, (2 * PAD, rows_of), 1)
        image = (row >= PAD).astype(jnp.int32)
        inside = row - image * PAD < SEQ
        hit = jnp.logical_and(inside, column == row - image * (PAD - SEQ))
        return jnp.where(hit, 1.0, 0.0).astype(BF16)

    def padded(ref):
        return dot(placement(), ref[...]).astype(BF16).reshape(2, 2, HALF, D)

    def norm_rows(s, v):
        return (normalize(v)[0] * gain[s : s + 1] + bias[s : s + 1]).astype(BF16)

    mo[...] = padded(tokens)
    for i in range(2):
        for half in range(2):
            n0[i, half] = norm_rows(0, mo[i, half].astype(F32))
        streams[0, i] = mo[i, core].astype(F32)

    def rows(ref, i):
        return ref[i].reshape(PAD, D)

    def block(s, i):
        if s != 1:
            return attention_forward(rows((n0, None, n2)[s], i), win, wout, s // 2, i, qkv, att, probs)
        loads.need("m1", "m2")
        hidden = dot(rows(n1, i), m1[...])
        act[i], dgelu[i] = gelu_pair(hidden)
        return dot(act[i], m2[...])

    normed = (n0, n1, n2, n3)

    def finish_forward(s, i):
        v = streams[s, i] + links.total(i, s % 2)
        streams[s + 1, i] = v
        normed[s + 1][i, core] = norm_rows(s + 1, v)
        links.gather((s, i), 2 * s + i, normed[s + 1].at[i])

    def hits():
        kept_choice = slots[...] < CAPACITY
        index = jnp.where(kept_choice, routes[...] * SLOTS + slots[...], -1)
        number = lax.broadcasted_iota(jnp.int32, (EXPERTS * SLOTS, rows_of), 0)
        return [number == index[k : k + 1] for k in range(2)]

    def make_pick():
        first, second = hits()
        flat = jnp.where(jnp.logical_or(first, second), 1.0, 0.0).astype(BF16)
        pick[...] = dot_nt(flat, placement()).astype(BF16)

    def make_spread():
        first, second = hits()
        flat = jnp.where(jnp.logical_or(first, second), 1.0, 0.0).astype(BF16)
        spread[...] = dot_nt(placement(), flat).astype(BF16)

    def make_gate():
        gate[...] = sum(
            jnp.sum(jnp.where(hit, gates[k : k + 1], 0.0), axis=1, keepdims=True)
            for k, hit in enumerate(hits())
        )

    def make_cot():
        cotp[...] = padded(cot)

    def make_drow():
        drow[...] = (dot(pick[...], cotp[...].reshape(2 * PAD, D)) * gate[...]).astype(BF16)

    fill = (make_pick, make_spread, make_gate, make_cot, make_drow, None)
    steps = [(s, i) for s in range(3) for i in range(2)]
    for at, (s, i) in enumerate(steps):
        if s > 0:
            links.arrived((s - 1, i))
        term = block(s, i)
        if at == 0:
            pl.semaphore_wait(barrier, 9)
        links.share(i, term)
        if fill[at] is not None:
            fill[at]()
        links.swap(i, s % 2)
        if at > 0:
            finish_forward(*steps[at - 1])
    finish_forward(*steps[-1])

    for i in range(2):
        links.arrived((2, i))
    buf[...] = dot(pick[...], n3[...].reshape(2 * PAD, D)).astype(BF16)
    for e in range(EXPERTS):
        cut = pl.ds(e * SLOTS, SLOTS)
        loads.need(("in", e), ("out", e))
        w_in = g[2 * (e % 2)].reshape(D, D)
        w_out = g[2 * (e % 2) + 1].reshape(D, D)
        a, slope = gelu_pair(dot(buf[cut], w_in))
        d = (slope * dot_nt(drow[cut], w_out)).astype(BF16)
        weighted[cut] = (dot(a, w_out) * gate[cut]).astype(BF16)
        dbuf[cut] = dot_nt(d, w_in).astype(BF16)
        weight_grad(ge, e, buf[cut], d)
        weight_grad(ge, EXPERTS + e, drow[cut], a)
        if e + 2 < EXPERTS:
            fetch(e + 2)
        if e == 1:
            groups["eay"].start(ge.at[0:2])
            groups["eaz"].start(ge.at[4:6])
        if e == 3:
            groups["eby"].start(ge.at[2:4])
            groups["ebz"].start(ge.at[6:8])
    dn[...] = dot(spread[...], dbuf[...]).astype(BF16).reshape(2, 2, HALF, D)
    for i in range(2):
        links.share_held(i, dn.at[i])
    mo[...] = dot(spread[...], weighted[...]).astype(BF16).reshape(2, 2, HALF, D)

    def flat(ref):
        return ref[...].reshape(2 * PAD, D)

    def share(parity, i, value):
        links.share(i, value)
        links.swap(i, parity)

    def finish(s, parity, i, base, target, slot):
        dv, gain_term, bias_term = norm_back(streams[s, i], gain[s : s + 1], links.total(i, parity))
        sums[s : s + 1] = sums[s : s + 1] + gain_term
        sums[4 + s : 5 + s] = sums[4 + s : 5 + s] + bias_term
        v = base[i].astype(F32) + dv if s < 3 else base[i, core].astype(F32) + dv
        if s > 0:
            g2[i] = v
            target[i, core] = v.astype(BF16)
        else:
            target[i, core] = v
        links.gather((s, i), 2 * slot + i, target.at[i])

    sums[...] = jnp.zeros_like(sums)
    for i in range(2):
        links.swap(i, 1)
    for i in range(2):
        links.share_held(2 + i, mo.at[i])
    for i in range(2):
        finish(3, 1, i, cotp, du2, 0)
    for i in range(2):
        links.swap(2 + i, 0)

    for i in range(2):
        links.arrived((3, i))
        share(0, i, attention_backward(rows(du2, i), win, wout, 1, i, qkv, att, probs, stack))
    for name in ("eay", "eaz"):
        groups[name].middle()
    head_grad(g, 3, flat(n2), flat(du2), stack)
    groups["a1y"].start(g.at[3:4, :, :, :, 0:384])
    groups["a1z"].start(g.at[3:4, :, :, :, 384:768])
    for i in range(2):
        finish(2, 0, i, g2, du1, 1)
    for i in range(2):
        out_o[i, core] = streams[3, i] + links.total(2 + i, 0)
        links.gather((4, i), 8 + i, out_o.at[i])

    for i in range(2):
        links.arrived((2, i))
        d = (dgelu[i] * dot_nt(rows(du1, i), m2[...])).astype(BF16)
        dhid[pl.ds(i * PAD, PAD)] = d
        share(1, i, dot_nt(d, m1[...]))
    for name in ("eby", "ebz"):
        groups[name].middle()
    weight_grad(g, 0, flat(n1), dhid[0 : 2 * PAD])
    groups["m0"].start(g.at[0:1])
    weight_grad(g, 1, flat(du1), act[...].reshape(2 * PAD, D))
    groups["m1"].start(g.at[1:2])
    for i in range(2):
        finish(1, 1, i, g2, du0, 2)

    for i in range(2):
        links.arrived((1, i))
        share(0, i, attention_backward(rows(du0, i), win, wout, 0, i, qkv, att, probs, stack))
    for name in ("eay", "eaz"):
        groups[name].second()
    head_grad(g, 2, flat(n0), flat(du0), stack)
    groups["a0y"].start(g.at[2:3, :, :, :, 0:384])
    groups["a0z"].start(g.at[2:3, :, :, :, 384:768])
    for i in range(2):
        finish(0, 0, i, g2, token_o, 3)
    both = links.copy(sums, sums_in, 20, links.other)
    for name in ("m0", "m1"):
        groups[name].middle()
    for name in ("a1y", "a1z", "eby", "ebz"):
        groups[name].second()
    both.wait()
    wide = jnp.concatenate([sums[...] + sums_in[...], jnp.zeros((120, D), F32)], axis=0)
    gn[0] = wide.T.astype(BF16).reshape(4, 4, 48, 128)
    groups["n"].start(gn)
    for name in ("eay", "eaz"):
        groups[name].third()
    for name in ("a0y", "a0z", "m0", "m1", "n"):
        groups[name].second()
    last = ("a1y", "a1z", "eby", "ebz", "a0y", "a0z", "m0", "m1", "n")
    for name in last:
        groups[name].third()
    for name in ("eay", "eaz") + last:
        groups[name].finish()
    for i in range(2):
        links.arrived((0, i))
        links.arrived((4, i))


def publish_kernel(*refs):
    count = (len(refs) - 3) // 2
    pads, sems = refs[-3:-1], refs[-1]
    targets = list(pads) + list(refs[count + 2 : 2 * count])
    copies = [pltpu.make_async_copy(refs[k], targets[k], sems.at[k]) for k in range(count)]
    for copy in copies:
        copy.start()
    for k in range(2):
        copies[k].wait()
        for i in range(2):
            refs[count + k][i * SEQ : (i + 1) * SEQ] = pads[k][i].reshape(PAD, D)[:SEQ]
    for copy in copies[2:]:
        copy.wait()


def link_scratch(channels, sems):
    return [
        pltpu.VMEM((2, HALF, D), F32),
        pltpu.VMEM((2, HALF, D), BF16),
        pltpu.VMEM((channels, HALF, D), BF16),
        pltpu.VMEM((channels, HALF, D), BF16),
        pltpu.VMEM((2 + channels, HALF, D), BF16),
        pltpu.SemaphoreType.DMA((sems,)),
        pltpu.SemaphoreType.DMA((sems,)),
    ]


def local(
    tokens,
    norm_gain,
    norm_bias,
    attn_in,
    attn_out,
    mlp_in,
    mlp_out,
    expert_in,
    expert_out,
    routes,
    slot_index,
    gate_weights,
    cotangent,
):
    head_width = attn_out.shape[1]
    slots = EXPERTS * SLOTS
    rows = tokens.shape[0]
    whole = pl.BlockSpec(memory_space=pltpu.VMEM)
    hbm = pl.BlockSpec(memory_space=pl.ANY)
    shape = jax.ShapeDtypeStruct
    half_rows = (2, 2, HALF, D)
    win = jnp.swapaxes(attn_in, 2, 3).reshape(6, head_width, D)
    scratch = (
        [pltpu.VMEM(half_rows, BF16)] * 7
        + [
            pltpu.VMEM((2, 3, 2, PAD, head_width), BF16),
            pltpu.VMEM((2, 2, PAD, head_width), BF16),
            pltpu.VMEM((2, 2, 3, PAD, PAD), BF16),
            pltpu.VMEM((2, PAD, D), BF16),
            pltpu.VMEM((2, PAD, D), F32),
            pltpu.VMEM((4, 2, HALF, D), F32),
            pltpu.VMEM((2, HALF, D), F32),
            pltpu.VMEM((slots, 2 * PAD), BF16),
            pltpu.VMEM((2 * PAD, slots), BF16),
            pltpu.VMEM((slots, 1), F32),
        ]
        + [pltpu.VMEM((slots, D), BF16)] * 4
        + [
            pltpu.VMEM((D, D), BF16),
            pltpu.VMEM((D, D), BF16),
            pltpu.VMEM((4, 4, 4, 48, D), BF16),
            pltpu.VMEM((2 * EXPERTS, 4, 4, 48, D), BF16),
            pltpu.VMEM((1, 4, 4, 48, 128), BF16),
            pltpu.VMEM((8, D), F32),
            pltpu.VMEM((8, D), F32),
        ]
        + link_scratch(4, 22)
        + [
            pltpu.SemaphoreType.DMA((10 * len(GROUPS),)),
            pltpu.SemaphoreType.DMA((10 * len(GROUPS),)),
            pltpu.SemaphoreType.DMA((10,)),
        ]
    )
    for spec in GROUPS.values():
        scratch += list(group_scratch(spec).values())
    results = pl.pallas_call(
        layers_kernel,
        out_shape=[
            shape(half_rows, F32),
            shape(half_rows, F32),
            shape((4, 24), F32),
            shape((4, 24), F32),
            shape((2, 3, 24, head_width), F32),
            shape((2, 24, head_width), F32),
            shape((24, D), F32),
            shape((24, D), F32),
            shape((EXPERTS, 24, D), F32),
            shape((EXPERTS, 24, D), F32),
        ],
        in_specs=[whole] * 9 + [hbm] * 4,
        out_specs=[whole] * 10,
        scratch_shapes=scratch,
        compiler_params=pltpu.CompilerParams(
            collective_id=1, has_side_effects=True, vmem_limit_bytes=63 << 20
        ),
        name="layers",
    )(
        tokens, cotangent, routes.T, slot_index.T, gate_weights.T, norm_gain, norm_bias, win, attn_out,
        mlp_in, mlp_out, expert_in.reshape(EXPERTS, 4, 4, 48, D), expert_out.reshape(EXPERTS, 4, 4, 48, D),
    )
    out, token_grad, gains, biases, heads_in, heads_out, m_in, m_out, e_in, e_out = pl.pallas_call(
        publish_kernel,
        out_shape=[shape((rows, D), F32)] * 2 + [shape(r.shape, r.dtype) for r in results[2:]],
        in_specs=[hbm] * len(results),
        out_specs=[whole] * len(results),
        scratch_shapes=[pltpu.VMEM(half_rows, F32)] * 2 + [pltpu.SemaphoreType.DMA((len(results),))],
        name="publish",
    )(*results)
    return (
        out,
        token_grad,
        gains,
        biases,
        heads_in,
        jnp.swapaxes(heads_out, 1, 2),
        m_in,
        m_out.T,
        e_in,
        jnp.swapaxes(e_out, 1, 2),
    )


def solution(mesh):
    placed = (
        P("dp", None),
        P(),
        P(),
        P(None, None, None, "tensor"),
        P(None, "tensor", None),
        P(None, "tensor"),
        P("tensor", None),
        P(None, None, "tensor"),
        P(None, "tensor", None),
        P("dp", None),
        P("dp", None),
        P("dp", None),
        P("dp", None),
    )
    return jax.shard_map(
        local,
        mesh=mesh,
        in_specs=placed,
        out_specs=(
            P("dp", None),
            P("dp", None),
            P(None, "dp"),
            P(None, "dp"),
            P(None, None, "dp", "tensor"),
            P(None, "tensor", "dp"),
            P("dp", "tensor"),
            P("tensor", "dp"),
            P(None, "dp", "tensor"),
            P(None, "tensor", "dp"),
        ),
        check_vma=False,
    )
```

time: 159 us -> 150 us (0.943)
  Pallas kernels: 158 us -> 149 us
    pallas_call x3 -> x2, Pallas kernels: 158 us -> 149 us  [the longest x1 145 us: local(): pl.pallas_call(layers_kernel, out_shape=[shape(half_rows, F32), shape(hal...]
where the time goes in v4:
time: 150 us
  Pallas kernels  149 us (99%)
    pallas_call x1, Pallas kernels, local(): pl.pallas_call(layers_kernel, out_shape=[shape(half_rows, F32), shape(hal...  145 us
    pallas_call x1, Pallas kernels, local(): pl.pallas_call(publish_kernel, out_shape=[shape((rows, D), F32)] * 2 + [s...  3.83 us

profile of v4, /device:TPU:0, one launch (start us, length us, event | category | flops | bytes accessed | tf_op | source)
XLA Modules:
  0.0 149.5 jit_solution(12436086973808468983)
XLA Ops:
  0.6 144.9 %layers.1 = (f32[2,2,112,768]{3,2,1,0:T(8,128)}, f32[2,2,112,768]{3,2,1,0:T(8,128)}, f32[4,24]{1,0:T(4,128)}, f32[4,24]{1,0:T(4,128)}, f32[2,3,24,192]{3,2,1,0:T...) custom-call(bf16[394,768]{1,0:T(8,128)(2,1)} %tokens.1, ...), custom_call_target="tpu_custom_call" | custom-call | tf_op jit(solution)/shard_map/layers/pallas_call | solution.py:721
  145.5 3.8 %publish.1 = (f32[394,768]{1,0:T(8,128)}, f32[394,768]{1,0:T(8,128)}, f32[4,24]{1,0:T(4,128)}, f32[4,24]{1,0:T(4,128)}, f32[2,3,24,192]{3,2,1,0:T(8,128)}, /*ind...) custom-call(f32[2,2,112,768]{3,2,1,0:T(8,128)} %get-tuple-element.30, ...), custom_call_target="tpu_custom_call" | custom-call | tf_op jit(solution)/shard_map/publish/pallas_call | solution.py:746
